TPU v7x, 32 devices: a whole 2x2x4 slice. The times are simulated.
32 devices in a mesh: dom: 8 (over z, core), st: 4 (over y, x).
Axes of the slice: x: 2, y: 2, z: 4, core: 2. Of those that a mesh axis runs over, the one named last changes fastest.
Arguments:
- orbitals: bfloat16 [384, 16384], P('st', 'dom')
- cell_matrix: bfloat16 [512, 512], replicated
- connectivity: int32 [128, 512], P('dom'), may hold values from 0 to 2303, as said below
- surface_nodes: int32 [8, 256], P('dom'), may hold values from 0 to 2047, as said below
- cell_scale: float32 [128], P('dom'), may hold values from 0.3 to 3
- potential: float32 [16384], P('dom'), may hold values from -1 to 2
Outputs:
- rotated_states: bfloat16 [384, 16384], P('st', 'dom')
Inputs may be any that keep to these rules, and one draw needn't show every extreme that they name: `connectivity`: within a cell all 512 numbers differ. In each domain the first 12 cells name only the domain's own nodes (numbers below 2048); the others may also name the 256 shared-surface nodes of the next domain. `surface_nodes`: each row names 256 different nodes.
All inputs are finite; a program needn't handle non-finite values.
Results may differ from a plain program's by a relative error of at most 0.002.
The roundings to bfloat16 on the way count: a program that leaves them out, or rounds other values in their place, can miss the bound.
Values may be sent and summed in bfloat16 or wider, within the bound.
A program may use at most 64 MiB of HBM per device.

v0:
```python
import jax
import jax.numpy as jnp
from jax import lax
from jax.sharding import PartitionSpec as P

DEGREE = 3
ROOT_ITERS = 4


center = 7.0
half_width = 6.0
epsilon = 1e-06


def from_behind(block, axis, distance):
    devices = range(lax.axis_size(axis))
    route = [(i - distance, i) for i in devices if i - distance in devices]
    return lax.ppermute(block, axis, route)


def apply_hamiltonian(values, connectivity, surface_ids, cell_scale, potential, cell_matrix):
    nodes_dev = values.shape[1]
    boundary = values[:, surface_ids]
    ghosts = from_behind(boundary, "dom", -1)
    extended = jnp.concatenate([values, ghosts], axis=1)
    gathered = extended[:, connectivity]
    products = jnp.dot(
        gathered.reshape(-1, gathered.shape[2]), cell_matrix, preferred_element_type=jnp.float32
    )
    products = products.reshape(gathered.shape) * cell_scale[None, :, None]
    totals = jnp.zeros(extended.shape, jnp.float32).at[:, connectivity].add(products)
    returned = from_behind(totals[:, nodes_dev:], "dom", 1)
    owned = totals[:, :nodes_dev].at[:, surface_ids].add(returned)
    return owned + potential[None, :] * values.astype(jnp.float32)


def newton_root(gram):
    highest = lax.Precision.HIGHEST
    states_all = gram.shape[0]
    scale_sum = jnp.sqrt(jnp.sum(gram * gram)) + epsilon
    identity = jnp.eye(states_all, dtype=jnp.float32)
    growing = gram / scale_sum
    inverse = identity
    for iteration in range(ROOT_ITERS):
        factor = 1.5 * identity - 0.5 * jnp.dot(inverse, growing, precision=highest)
        growing = jnp.dot(growing, factor, precision=highest)
        inverse = jnp.dot(factor, inverse, precision=highest)
    return (inverse, scale_sum)


def body(orbitals, cell_matrix, connectivity, surface_nodes, cell_scale, potential):
    surface_ids = surface_nodes[0]
    older = orbitals
    newest = orbitals
    for degree_step in range(DEGREE):
        image = apply_hamiltonian(
            newest, connectivity, surface_ids, cell_scale, potential, cell_matrix
        )
        shifted = (image - center * newest.astype(jnp.float32)) / half_width
        if degree_step == 0:
            fresh = shifted
        else:
            fresh = 2.0 * shifted - older.astype(jnp.float32)
        older = newest
        newest = fresh.astype(jnp.bfloat16)
    slabs = lax.all_to_all(newest, "st", split_axis=1, concat_axis=0, tiled=True)
    gram_part = jnp.dot(slabs, slabs.T, preferred_element_type=jnp.float32)
    row_block = lax.psum_scatter(gram_part, "st", scatter_dimension=0, tiled=True)
    row_block = lax.psum(row_block, "dom")
    gram = lax.all_gather(row_block, "st", axis=0, tiled=True)
    inverse, scale_sum = newton_root(gram)
    node_total = lax.axis_size("dom") * orbitals.shape[1]
    rotation = (inverse * jnp.sqrt(node_total / scale_sum)).astype(jnp.bfloat16)
    rotated = jnp.dot(rotation.T, slabs, preferred_element_type=jnp.float32).astype(jnp.bfloat16)
    return lax.all_to_all(rotated, "st", split_axis=0, concat_axis=1, tiled=True)


def solution(mesh):
    return jax.shard_map(
        body,
        mesh=mesh,
        in_specs=(P("st", "dom"), P(), P("dom", None), P("dom", None), P("dom"), P("dom")),
        out_specs=P("st", "dom"),
        check_vma=False,
    )
```

profile of v0, /device:TPU:0, one launch (start us, length us, event | category | flops | bytes accessed | tf_op | source)
XLA Modules:
  0.0 446.3 jit_solution(9668120416585132764)
XLA Ops:
  12.7 29.2 %gather_fusion.1 = bf16[8192,96]{1,0:T(8,128)(2,1)} fusion(bf16[96,2304]{0,1:T(8,128)(2,1)S(1)} %pad_maximum_fusion, s32[8192]{0:T(1024)S(1)} %broadcast_clamp_fusion), kind=kCustom, calls=%fused_computation.1 | custom fusion | bytes 3178496 | tf_op jit(solution)/shard_map/gather | solution.py:26
  41.9 3.2 copy.19
  47.8 5.0 %copy.28 = f32[16,512,96]{2,1,0:T(8,128)} copy(f32[16,512,96]{1,0,2:T(8,128)} %multiply_bitcast_fusion.2) | data formatting | bytes 6291456 | tf_op jit(solution)/shard_map/mul | solution.py:30
  52.8 44.6 %scatter_custom_fusion = f32[96,2304]{0,1:T(8,128)S(1)} fusion(s32[8192]{0:T(1024)S(1)} %bitcast.88, f32[8192,96]{1,0:T(8,128)} %bitcast.82, f32[]{:T(128)} %constant.12.clone.1), kind=kCustom, calls=%fused_computation.57 | custom fusion | flops 786432 | bytes 885248 | tf_op jit(solution)/shard_map/scatter-add | solution.py:31
  97.4 5.8 %collective-permute-start.1 = (f32[96,256]{0,1:T(8,128)S(1)}, f32[96,256]{0,1:T(8,128)S(1)}, u32[]{:S(2)}, u32[]{:S(2)}) collective-permute-start(f32[96,256]{0,1:T(8,128)S(1)} %slice.37), channel_id=1, source_target_pairs={{0,4},{4,8},{8,12},{12,16},{16,20},{20,24},{24,28},{1,5},{5,9},{9,... | collective-permute-start | bytes 294920 | tf_op jit(solution)/shard_map/ppermute | solution.py:18
  111.2 29.2 %gather_fusion.3 = bf16[8192,96]{1,0:T(8,128)(2,1)} fusion(bf16[96,2304]{0,1:T(8,128)(2,1)S(1)} %pad_maximum_fusion.1, s32[8192]{0:T(1024)S(1)} %broadcast_clamp_fusion), kind=kCustom, calls=%fused_computation.3 | custom fusion | bytes 3178496 | tf_op jit(solution)/shard_map/gather | solution.py:26
  140.5 3.2 copy.22
  143.7 2.7 multiply_bitcast_fusion.1
  146.3 5.0 %copy.29 = f32[16,512,96]{2,1,0:T(8,128)} copy(f32[16,512,96]{1,0,2:T(8,128)} %multiply_bitcast_fusion.1) | data formatting | bytes 6291456 | tf_op jit(solution)/shard_map/mul | solution.py:30
  151.3 44.6 %scatter_custom_fusion.2 = f32[96,2304]{0,1:T(8,128)S(1)} fusion(s32[8192]{0:T(1024)S(1)} %bitcast.89, f32[8192,96]{1,0:T(8,128)} %bitcast.83, f32[]{:T(128)} %constant.12.clone.1), kind=kCustom, calls=%fused_computation.55 | custom fusion | flops 786432 | bytes 885248 | tf_op jit(solution)/shard_map/scatter-add | solution.py:31
  195.9 5.6 %collective-permute-start.3 = (f32[96,256]{0,1:T(8,128)S(1)}, f32[96,256]{0,1:T(8,128)S(1)}, u32[]{:S(2)}, u32[]{:S(2)}) collective-permute-start(f32[96,256]{0,1:T(8,128)S(1)} %slice.39), channel_id=1, source_target_pairs={{0,4},{4,8},{8,12},{12,16},{16,20},{20,24},{24,28},{1,5},{5,9},{9,... | collective-permute-start | bytes 294920 | tf_op jit(solution)/shard_map/ppermute | solution.py:18
  202.8 4.0 scatter_custom_fusion.3
  212.5 29.2 %gather_fusion.5 = bf16[8192,96]{1,0:T(8,128)(2,1)} fusion(bf16[96,2304]{0,1:T(8,128)(2,1)S(1)} %pad_maximum_fusion.2, s32[8192]{0:T(1024)S(1)} %broadcast_clamp_fusion), kind=kCustom, calls=%fused_computation.5 | custom fusion | bytes 3178496 | tf_op jit(solution)/shard_map/gather | solution.py:26
  241.7 4.4 copy.24
  246.1 4.1 multiply_bitcast_fusion
  250.2 5.0 %copy.30 = f32[16,512,96]{2,1,0:T(8,128)} copy(f32[16,512,96]{1,0,2:T(8,128)} %multiply_bitcast_fusion) | data formatting | bytes 6291456 | tf_op jit(solution)/shard_map/mul | solution.py:30
  255.1 44.6 %scatter_custom_fusion.4 = f32[96,2304]{0,1:T(8,128)S(1)} fusion(s32[8192]{0:T(1024)S(1)} %bitcast.90, f32[8192,96]{1,0:T(8,128)} %bitcast.81, f32[]{:T(128)} %constant.12.clone.1), kind=kCustom, calls=%fused_computation.53 | custom fusion | flops 786432 | bytes 885248 | tf_op jit(solution)/shard_map/scatter-add | solution.py:31
  299.8 5.6 %collective-permute-start.5 = (f32[96,256]{0,1:T(8,128)S(1)}, f32[96,256]{0,1:T(8,128)S(1)}, u32[]{:S(2)}, u32[]{:S(2)}) collective-permute-start(f32[96,256]{0,1:T(8,128)S(1)} %slice.41), channel_id=1, source_target_pairs={{0,4},{4,8},{8,12},{12,16},{16,20},{20,24},{24,28},{1,5},{5,9},{9,... | collective-permute-start | bytes 294920 | tf_op jit(solution)/shard_map/ppermute | solution.py:18
  306.7 4.0 scatter_custom_fusion.5
  312.3 11.4 %all_to_all.38 = bf16[96,4,512]{2,0,1:T(8,128)(2,1)S(1)} all-to-all(bf16[96,4,512]{2,0,1:T(8,128)(2,1)S(1)} %copy.26), channel_id=1, replica_groups=mesh['dom'=8,'st'=4] {'st'}, dimensions={1} | all-to-all | bytes 786432 | tf_op jit(solution)/shard_map/all_to_all | solution.py:66
  325.0 24.8 %reduce-scatter.2.cloned.1.call-done = f32[96,384]{1,0:T(8,128)} async-done(((f32[384,384]{1,0:T(8,128)}), f32[96,384]{1,0:T(8,128)}) %reduce-scatter.2.cloned.1.call-update) | async-done | bytes 147472 | tf_op jit(solution)/shard_map/reduce_scatter | solution.py:68
  349.8 54.5 %all-reduce.2.cloned.1.call-done = f32[96,384]{1,0:T(8,128)} async-done(((f32[96,384]{1,0:T(8,128)}), f32[96,384]{1,0:T(8,128)}) %all-reduce.2.cloned.1.call-update) | async-done | bytes 147472 | tf_op jit(solution)/shard_map/psum | solution.py:69
  404.3 10.6 %all_gather.3 = f32[384,384]{1,0:T(8,128)S(1)} all-gather(f32[96,384]{1,0:T(8,128)} %all-reduce.2.cloned.1.call-done), channel_id=1, replica_groups=mesh['dom'=8,'st'=4] {'st'}, dimensions={0}, use_global_device_ids=true | all-gather | bytes 737280 | tf_op jit(solution)/shard_map/all_gather | solution.py:70
  429.7 9.0 %all_to_all.39 = bf16[4,96,512]{2,1,0:T(8,128)(2,1)S(1)} all-to-all(bf16[4,96,512]{2,1,0:T(8,128)(2,1)S(1)} %bitcast.85), channel_id=1, replica_groups=mesh['dom'=8,'st'=4] {'st'}, dimensions={0} | all-to-all | bytes 786432 | tf_op jit(solution)/shard_map/all_to_all | solution.py:75
  (58 shorter events, 42.9 us)
Async XLA Ops:
  6.5 38.6 %copy-start = (bf16[512,512]{1,0:T(8,128)(2,1)S(1)}, bf16[512,512]{1,0:T(8,128)(2,1)}, u32[]{:S(2)}) copy-start(bf16[512,512]{1,0:T(8,128)(2,1)} %param.7) | copy-start | bytes 1572868
  6.5 343.3 %reduce-scatter.2.cloned.1.call-start = ((), (), s32[]{:S(2)}) async-start(), calls=%async_computation.3 | async-start | bytes 737280 | tf_op jit(solution)/shard_map/reduce_scatter | solution.py:68
  9.4 3.1 collective-permute-start
  41.9 3.2 copy-start.2
  47.8 55.4 %copy-start.1 = (f32[2048]{0:T(1024)S(1)}, f32[2048]{0:T(1024)}, u32[]{:S(2)}) copy-start(f32[2048]{0:T(1024)} %param.11) | copy-start | bytes 24580
  97.4 6.7 %collective-permute-start.1 = (f32[96,256]{0,1:T(8,128)S(1)}, f32[96,256]{0,1:T(8,128)S(1)}, u32[]{:S(2)}, u32[]{:S(2)}) collective-permute-start(f32[96,256]{0,1:T(8,128)S(1)} %slice.37), channel_id=1, source_target_pairs={{0,4},{4,8},{8,12},{12,16},{16,20},{20,24},{24,28},{1,5},{5,9},{9,... | collective-permute-start | bytes 294920 | tf_op jit(solution)/shard_map/ppermute | solution.py:18
  107.5 3.6 collective-permute-start.2
  195.9 6.9 %collective-permute-start.3 = (f32[96,256]{0,1:T(8,128)S(1)}, f32[96,256]{0,1:T(8,128)S(1)}, u32[]{:S(2)}, u32[]{:S(2)}) collective-permute-start(f32[96,256]{0,1:T(8,128)S(1)} %slice.39), channel_id=1, source_target_pairs={{0,4},{4,8},{8,12},{12,16},{16,20},{20,24},{24,28},{1,5},{5,9},{9,... | collective-permute-start | bytes 294920 | tf_op jit(solution)/shard_map/ppermute | solution.py:18
  209.1 3.2 collective-permute-start.4
  299.8 6.9 %collective-permute-start.5 = (f32[96,256]{0,1:T(8,128)S(1)}, f32[96,256]{0,1:T(8,128)S(1)}, u32[]{:S(2)}, u32[]{:S(2)}) collective-permute-start(f32[96,256]{0,1:T(8,128)S(1)} %slice.41), channel_id=1, source_target_pairs={{0,4},{4,8},{8,12},{12,16},{16,20},{20,24},{24,28},{1,5},{5,9},{9,... | collective-permute-start | bytes 294920 | tf_op jit(solution)/shard_map/ppermute | solution.py:18
  324.9 79.3 %all-reduce.2.cloned.1.call-start = ((), (), s32[]{:S(2)}) async-start(), calls=%async_computation.4 | async-start | bytes 294912 | tf_op jit(solution)/shard_map/psum | solution.py:69
Sparse Core Ops, SparseCore 0:
  325.1 24.6 reduce-scatter.1
  352.2 52.0 all-reduce.1
where the time goes:
time: 448 us; the launch traced here: 446 us
  other arithmetic  153 us (34%)
  local copies, waits for them, and re-layouts  118 us (26%)
  waiting for transfers between devices  85.2 us (19%)
  blocking collectives  30.9 us (7%)
  matrix products  23.8 us (5%)
  starting transfers between devices  20.8 us (5%)
  between operations  14.5 us (3%)
    scatter-add x3, other arithmetic, apply_hamiltonian(): jnp.zeros(extended.shape, jnp.float32).at[:, connectivity].add(products)  134 us
    gather x6, local copies, waits for them, and re-layouts, apply_hamiltonian(): gathered = extended[:, connectivity]  98.4 us
    psum x1, waiting for transfers between devices, body(): row_block = lax.psum(row_block, 'dom')  54.5 us
    reduce_scatter x1, waiting for transfers between devices, body(): lax.psum_scatter(gram_part, 'st', scatter_dimension=0, tiled=True)  24.8 us
    ppermute x6, starting transfers between devices, from_behind(): return lax.ppermute(block, axis, route)  20.7 us
    mul x3, local copies, waits for them, and re-layouts, apply_hamiltonian(): products = products.reshape(gathered.shape) * cell_scale[None, :, None]  14.9 us
    all_to_all x1, blocking collectives, body(): lax.all_to_all(newest, 'st', split_axis=1, concat_axis=0, tiled=True)  11.4 us
    all_gather x1, blocking collectives, body(): gram = lax.all_gather(row_block, 'st', axis=0, tiled=True)  10.6 us
  transfers between devices with their start and end apart: 8, of which 6 were waited for; matrix products, arithmetic and copies ran while one was open for 1% of the time, Pallas kernels for 0%

commit v1 on v0

v1 whole, which is shorter than its diff:
```python
import functools

import jax
import jax.numpy as jnp
from jax import lax
from jax.experimental import pallas as pl
from jax.experimental.pallas import tpu as pltpu
from jax.sharding import PartitionSpec as P

DEGREE = 3
ROOT_ITERS = 4
MESH = pl.DeviceIdType.MESH

center = 7.0
half_width = 6.0
epsilon = 1e-06

NT = (((1,), (1,)), ((), ()))


def halves(values):
    high = values.astype(jnp.bfloat16)
    low = (values - high.astype(jnp.float32)).astype(jnp.bfloat16)
    return jnp.concatenate([high, low], axis=0)


def filter_kernel(
    n_dom, inner,
    f_ref, matrix_ref, conn_ref, surface_ref, scale_ref, potential_ref, out_ref,
    extended, middle, totals, picks, surface_pick, pair, edge_out, edge_in, back_out, back_in,
    edge_send, edge_recv, back_send, back_recv,
):
    states, nodes = f_ref.shape
    surf = surface_ref.shape[1]
    cells = conn_ref.shape[0]
    width = nodes + surf
    tile = 256
    me = lax.axis_index("dom")
    after, before = lax.rem(me + 1, n_dom), lax.rem(me + n_dom - 1, n_dom)

    barrier = pltpu.get_barrier_semaphore()
    for neighbour in (after, before):
        pl.semaphore_signal(barrier, inc=1, device_id={"dom": neighbour}, device_id_type=MESH)

    def one_hot(ids, start, rows):
        node = start + lax.broadcasted_iota(jnp.int32, (rows, ids.shape[1]), 0)
        return jnp.where(node == ids, 1.0, 0.0).astype(jnp.bfloat16)

    for start in range(0, nodes, tile):
        surface_pick[pl.ds(start, tile), :] = one_hot(surface_ref[...], start, tile)

    def add_back(parts, pick, start, rows):
        spread = lax.dot_general(parts, pick, NT, preferred_element_type=jnp.float32)
        totals[:, pl.ds(start, rows)] += spread[:states] + spread[states:]

    def run_cells(first, last, extent, build):
        def one_cell(cell, carry):
            if build:
                ids = conn_ref[pl.ds(cell, 1), :]
                for start in range(0, extent, tile):
                    picks[cell, pl.ds(start, tile), :] = one_hot(ids, start, tile)
            gathered = jnp.dot(
                extended[:, :extent], picks[cell, :extent, :], preferred_element_type=jnp.float32
            ).astype(jnp.bfloat16)
            products = jnp.dot(gathered, matrix_ref[...], preferred_element_type=jnp.float32)
            pair[...] = halves(products * scale_ref[cell])
            for start in range(0, extent, tile):
                add_back(pair[...], picks[cell, pl.ds(start, tile), :], start, tile)
            return carry

        lax.fori_loop(first, last, one_cell, 0)

    extended[:, :nodes] = f_ref[...]
    for step in range(DEGREE):
        edge_out[step] = jnp.dot(
            extended[:, :nodes], surface_pick[...], preferred_element_type=jnp.float32
        ).astype(jnp.bfloat16)
        if step == 0:
            pl.semaphore_wait(barrier, 2)
        edge = pltpu.make_async_remote_copy(
            src_ref=edge_out.at[step], dst_ref=edge_in.at[step],
            send_sem=edge_send.at[step], recv_sem=edge_recv.at[step],
            device_id={"dom": before}, device_id_type=MESH,
        )
        edge.start()
        totals[...] = jnp.zeros_like(totals)
        run_cells(0, inner // 2, nodes, step == 0)
        edge.wait()
        ghosts = edge_in[step]
        extended[:, nodes:] = jnp.where(me == n_dom - 1, jnp.zeros_like(ghosts), ghosts)
        run_cells(inner, cells, width, step == 0)
        back_out[step] = totals[:, nodes:]
        back = pltpu.make_async_remote_copy(
            src_ref=back_out.at[step], dst_ref=back_in.at[step],
            send_sem=back_send.at[step], recv_sem=back_recv.at[step],
            device_id={"dom": after}, device_id_type=MESH,
        )
        back.start()
        run_cells(inner // 2, inner, nodes, step == 0)
        back.wait()
        returned = back_in[step]
        returned = jnp.where(me == 0, jnp.zeros_like(returned), returned)
        parts = halves(returned)
        for start in range(0, nodes, tile):
            add_back(parts, surface_pick[pl.ds(start, tile), :], start, tile)
        for start in range(0, nodes, tile):
            columns = pl.ds(start, tile)
            newest = extended[:, columns].astype(jnp.float32)
            image = totals[:, columns] + potential_ref[:, columns] * newest
            fresh = (image - center * newest) / half_width
            if step > 0:
                older = f_ref if step == 1 else middle
                fresh = 2.0 * fresh - older[:, columns].astype(jnp.float32)
            fresh = fresh.astype(jnp.bfloat16)
            if step == DEGREE - 1:
                out_ref[:, columns] = fresh
            else:
                extended[:, columns] = fresh
                if step == 0:
                    middle[:, columns] = fresh


def filtered_states(orbitals, cell_matrix, connectivity, surface_nodes, cell_scale, potential):
    states, nodes = orbitals.shape
    cells, node_cell = connectivity.shape
    surf = surface_nodes.shape[1]
    vmem = pl.BlockSpec(memory_space=pltpu.VMEM)
    smem = pl.BlockSpec(memory_space=pltpu.SMEM)
    bf16, f32 = jnp.bfloat16, jnp.float32
    return pl.pallas_call(
        functools.partial(filter_kernel, lax.axis_size("dom"), cells - cells // 4),
        out_shape=jax.ShapeDtypeStruct((states, nodes), bf16),
        in_specs=[vmem, vmem, vmem, vmem, smem, vmem],
        out_specs=vmem,
        scratch_shapes=[
            pltpu.VMEM((states, nodes + surf), bf16),
            pltpu.VMEM((states, nodes), bf16),
            pltpu.VMEM((states, nodes + surf), f32),
            pltpu.VMEM((cells, nodes + surf, node_cell), bf16),
            pltpu.VMEM((nodes, surf), bf16),
            pltpu.VMEM((2 * states, node_cell), bf16),
            pltpu.VMEM((DEGREE, states, surf), bf16),
            pltpu.VMEM((DEGREE, states, surf), bf16),
            pltpu.VMEM((DEGREE, states, surf), f32),
            pltpu.VMEM((DEGREE, states, surf), f32),
        ] + [pltpu.SemaphoreType.DMA((DEGREE,))] * 4,
        compiler_params=pltpu.CompilerParams(
            collective_id=0, has_side_effects=True, vmem_limit_bytes=52 * 1024 * 1024
        ),
        name="chebyshev_filter",
    )(orbitals, cell_matrix, connectivity, surface_nodes, cell_scale, potential[None, :])


def newton_root(gram):
    highest = lax.Precision.HIGHEST
    states_all = gram.shape[0]
    scale_sum = jnp.sqrt(jnp.sum(gram * gram)) + epsilon
    identity = jnp.eye(states_all, dtype=jnp.float32)
    growing = gram / scale_sum
    inverse = identity
    for iteration in range(ROOT_ITERS):
        factor = 1.5 * identity - 0.5 * jnp.dot(inverse, growing, precision=highest)
        growing = jnp.dot(growing, factor, precision=highest)
        inverse = jnp.dot(factor, inverse, precision=highest)
    return (inverse, scale_sum)


def body(orbitals, cell_matrix, connectivity, surface_nodes, cell_scale, potential):
    newest = filtered_states(
        orbitals, cell_matrix, connectivity, surface_nodes, cell_scale, potential
    )
    slabs = lax.all_to_all(newest, "st", split_axis=1, concat_axis=0, tiled=True)
    gram_part = jnp.dot(slabs, slabs.T, preferred_element_type=jnp.float32)
    row_block = lax.psum_scatter(gram_part, "st", scatter_dimension=0, tiled=True)
    row_block = lax.psum(row_block, "dom")
    gram = lax.all_gather(row_block, "st", axis=0, tiled=True)
    inverse, scale_sum = newton_root(gram)
    node_total = lax.axis_size("dom") * orbitals.shape[1]
    rotation = (inverse * jnp.sqrt(node_total / scale_sum)).astype(jnp.bfloat16)
    rotated = jnp.dot(rotation.T, slabs, preferred_element_type=jnp.float32).astype(jnp.bfloat16)
    return lax.all_to_all(rotated, "st", split_axis=0, concat_axis=1, tiled=True)


def solution(mesh):
    return jax.shard_map(
        body,
        mesh=mesh,
        in_specs=(P("st", "dom"), P(), P("dom", None), P("dom", None), P("dom"), P("dom")),
        out_specs=P("st", "dom"),
        check_vma=False,
    )
```

time: 448 us -> 221 us (0.49)
  other arithmetic: 153 us -> 0.75 us
  local copies, waits for them, and re-layouts: 118 us -> 4.99 us
  Pallas kernels: 0 us -> 78.1 us
  starting transfers between devices: 20.8 us -> 0.04 us
  matrix products: 23.8 us -> 14.4 us
  waiting for transfers between devices: 85.2 us -> 77.8 us
    scatter-add x6 -> x0, other arithmetic: 144 us -> none  [the longest x3 134 us: apply_hamiltonian(): jnp.zeros(extended.shape, jnp.float32).at[:, connectivity].add(products)]
    gather x9 -> x0, local copies, waits for them, and re-layouts: 101 us -> none  [the longest x6 98.4 us: apply_hamiltonian(): gathered = extended[:, connectivity]]
    pallas_call x0 -> x1, Pallas kernels: none -> 78.1 us  [filtered_states(): pl.pallas_call(functools.partial(filter_kernel, lax.axis_size('dom'), cel...]
    ppermute x6 -> x0, starting transfers between devices: 20.7 us -> none  [from_behind(): return lax.ppermute(block, axis, route)]
    mul x3 -> x0, local copies, waits for them, and re-layouts: 14.9 us -> none  [apply_hamiltonian(): products = products.reshape(gathered.shape) * cell_scale[None, :, None]]
    dot_general x3 -> x0, matrix products: 9.38 us -> none  [apply_hamiltonian(): jnp.dot(gathered.reshape(-1, gathered.shape[2]), cell_matrix, preferred_e...]
    ppermute x6 -> x0, waiting for transfers between devices: 5.95 us -> none  [from_behind(): return lax.ppermute(block, axis, route)]
  transfers between devices with their start and end apart: 8 -> 2, of which waited for: 6 -> 2; matrix products, arithmetic and copies ran while one was open for 1% -> 0% of each run, Pallas kernels for 0% -> 0%
where the time goes in v1:
time: 221 us; the launch traced here: 220 us
  Pallas kernels  78.1 us (35%)
  waiting for transfers between devices  77.8 us (35%)
  blocking collectives  29.7 us (13%)
  matrix products  14.4 us (7%)
  between operations  14.3 us (6%)
  local copies, waits for them, and re-layouts  4.99 us (2%)
    pallas_call x1, Pallas kernels, filtered_states(): pl.pallas_call(functools.partial(filter_kernel, lax.axis_size('dom'), cel...  78.1 us
    psum x1, waiting for transfers between devices, body(): row_block = lax.psum(row_block, 'dom')  54.5 us
    reduce_scatter x1, waiting for transfers between devices, body(): lax.psum_scatter(gram_part, 'st', scatter_dimension=0, tiled=True)  23.3 us
    all_gather x1, blocking collectives, body(): gram = lax.all_gather(row_block, 'st', axis=0, tiled=True)  10.8 us
    all_to_all x1, blocking collectives, body(): lax.all_to_all(newest, 'st', split_axis=1, concat_axis=0, tiled=True)  9.94 us
    all_to_all x1, blocking collectives, body(): lax.all_to_all(rotated, 'st', split_axis=0, concat_axis=1, tiled=True)  8.96 us
    dot_general x4, matrix products, newton_root(): factor = 1.5 * identity - 0.5 * jnp.dot(inverse, growing, precision=highest)  4.58 us
    dot_general x4, matrix products, newton_root(): inverse = jnp.dot(factor, inverse, precision=highest)  4.45 us
  transfers between devices with their start and end apart: 2, of which 2 were waited for; matrix products, arithmetic and copies ran while one was open for 0% of the time, Pallas kernels for 0%

profile of v1, /device:TPU:0, one launch (start us, length us, event | category | flops | bytes accessed | tf_op | source)
XLA Modules:
  0.0 220.1 jit_solution(14993541359563764733)
XLA Ops:
  7.2 1.0 copy-done
  8.3 1.0 copy-done.1
  9.3 0.8 copy-done.2
  10.0 0.7 copy-done.3
  10.7 78.1 %chebyshev_filter.1 = bf16[96,2048]{1,0:T(8,128)(2,1)S(1)} custom-call(bf16[96,2048]{1,0:T(8,128)(2,1)S(1)} %copy-done.1, bf16[512,512]{1,0:T(8,128)(2,1)S(1)} %copy-done, s32[16,512]{1,0:T(8,128)S(1)} %copy-done.2, s32[1,256]{1,0:T(1,128)S(1)} %copy-done.4, f32[16]{0:T(128)S(1)} %copy-done.5, f32[1,2048]{1,0:T(1,128)S(1)} %bitcast.35), custom_call_target="tpu_custom_call" | custom-call | tf_op jit(solution)/shard_map/chebyshev_filter/pallas_call | solution.py:130
  88.9 9.9 %all_to_all.38 = bf16[96,4,512]{2,0,1:T(8,128)(2,1)S(1)} all-to-all(bf16[96,4,512]{2,0,1:T(8,128)(2,1)S(1)} %bitcast.39), channel_id=1, replica_groups=mesh['dom'=8,'st'=4] {'st'}, dimensions={1} | all-to-all | bytes 786432 | tf_op jit(solution)/shard_map/all_to_all | solution.py:172
  98.8 1.2 fusion.7
  100.1 23.3 %reduce-scatter.2.cloned.1.call-done = f32[96,384]{1,0:T(8,128)} async-done(((f32[384,384]{1,0:T(8,128)}), f32[96,384]{1,0:T(8,128)}) %reduce-scatter.2.cloned.1.call-update) | async-done | bytes 147472 | tf_op jit(solution)/shard_map/reduce_scatter | solution.py:174
  123.5 54.5 %all-reduce.2.cloned.1.call-done = f32[96,384]{1,0:T(8,128)} async-done(((f32[96,384]{1,0:T(8,128)}), f32[96,384]{1,0:T(8,128)}) %all-reduce.2.cloned.1.call-update) | async-done | bytes 147472 | tf_op jit(solution)/shard_map/psum | solution.py:175
  177.9 10.8 %all_gather.3 = f32[384,384]{1,0:T(8,128)S(1)} all-gather(f32[96,384]{1,0:T(8,128)} %all-reduce.2.cloned.1.call-done), channel_id=1, replica_groups=mesh['dom'=8,'st'=4] {'st'}, dimensions={0}, use_global_device_ids=true | all-gather | bytes 737280 | tf_op jit(solution)/shard_map/all_gather | solution.py:176
  188.7 0.8 multiply_reduce_fusion
  190.2 0.8 fusion.3
  190.9 1.3 fusion.6
  192.2 0.7 fusion.5
  192.9 1.3 fusion
  194.1 1.3 fusion.9
  195.4 1.3 fusion.8
  196.7 1.3 fusion.1
  198.0 1.3 fusion.10
  199.3 1.3 fusion.11
  200.6 1.3 fusion.2
  201.9 1.3 fusion.4
  203.6 9.0 %all_to_all.39 = bf16[4,96,512]{2,1,0:T(8,128)(2,1)S(1)} all-to-all(bf16[4,96,512]{2,1,0:T(8,128)(2,1)S(1)} %bitcast.38), channel_id=1, replica_groups=mesh['dom'=8,'st'=4] {'st'}, dimensions={0} | all-to-all | bytes 786432 | tf_op jit(solution)/shard_map/all_to_all | solution.py:181
  212.5 0.8 copy.11
  (14 shorter events, 1.2 us)
Async XLA Ops:
  6.5 0.7 copy-start.5
  6.5 0.7 copy-start.4
  6.5 116.9 %reduce-scatter.2.cloned.1.call-start = ((), (), s32[]{:S(2)}) async-start(), calls=%async_computation.3 | async-start | bytes 737280 | tf_op jit(solution)/shard_map/reduce_scatter | solution.py:174
  7.2 1.0 copy-start
  8.3 1.0 copy-start.1
  9.3 0.8 copy-start.2
  10.0 0.7 copy-start.3
  100.1 77.9 %all-reduce.2.cloned.1.call-start = ((), (), s32[]{:S(2)}) async-start(), calls=%async_computation.4 | async-start | bytes 294912 | tf_op jit(solution)/shard_map/psum | solution.py:175
Sparse Core Ops, SparseCore 0:
  100.2 23.2 reduce-scatter.1
  125.9 52.0 all-reduce.1

commit v2 on v1

v2 whole, which is shorter than its diff:
```python
import functools

import jax
import jax.numpy as jnp
from jax import lax
from jax.experimental import pallas as pl
from jax.experimental.pallas import tpu as pltpu
from jax.sharding import PartitionSpec as P

DEGREE = 3
ROOT_ITERS = 4
MESH = pl.DeviceIdType.MESH

center = 7.0
half_width = 6.0
epsilon = 1e-06

NT = (((1,), (1,)), ((), ()))


def halves(values):
    high = values.astype(jnp.bfloat16)
    low = (values - high.astype(jnp.float32)).astype(jnp.bfloat16)
    return jnp.concatenate([high, low], axis=0)


def filter_kernel(
    n_dom, inner,
    f_ref, matrix_ref, conn_ref, surface_ref, scale_ref, potential_ref, out_ref,
    extended, history, totals, picks, surface_pick, pair, edge_out, edge_in, back_out, back_in,
    edge_send, edge_recv, back_send, back_recv,
):
    states, nodes = f_ref.shape
    surf = surface_ref.shape[1]
    cells, node_cell = conn_ref.shape
    width = nodes + surf
    tile = 256
    me = lax.axis_index("dom")
    after, before = lax.rem(me + 1, n_dom), lax.rem(me + n_dom - 1, n_dom)

    barrier = pltpu.get_barrier_semaphore()
    for neighbour in (after, before):
        pl.semaphore_signal(barrier, inc=1, device_id={"dom": neighbour}, device_id_type=MESH)

    def one_hot(ids, start):
        columns = ids.shape[1]
        node = lax.broadcasted_iota(jnp.int32, (tile, columns), 0).astype(jnp.bfloat16)
        wanted = jnp.broadcast_to((ids - start).astype(jnp.bfloat16), (tile, columns))
        one, zero = jnp.bfloat16(1), jnp.bfloat16(0)
        return jnp.where(node == wanted, one, zero)

    for start in range(0, nodes, tile):
        surface_pick[pl.ds(start, tile), :] = one_hot(surface_ref[...], start)
    for cell in range(cells):
        ids = conn_ref[pl.ds(cell, 1), :]
        lanes = pl.ds(cell * node_cell, node_cell)

        def build_tile(index, carry):
            start = index * tile
            picks[pl.ds(pl.multiple_of(start, tile), tile), lanes] = one_hot(ids, start)
            return carry

        lax.fori_loop(0, (nodes if cell < inner else width) // tile, build_tile, 0)

    def run_cells(first, last, extent):
        count = last - first
        gathered = []
        for cell in range(first, last):
            lanes = pl.ds(cell * node_cell, node_cell)
            gathered.append(jnp.dot(
                extended[:, :extent], picks[:extent, lanes], preferred_element_type=jnp.float32
            ).astype(jnp.bfloat16))
        products = jnp.dot(
            jnp.concatenate(gathered, axis=0), matrix_ref[...], preferred_element_type=jnp.float32
        )
        for index in range(count):
            scaled = products[index * states:(index + 1) * states] * scale_ref[first + index]
            pair[:, index * node_cell:(index + 1) * node_cell] = halves(scaled)
        group = pl.ds(first * node_cell, count * node_cell)

        def scatter_tile(index, carry):
            rows = pl.ds(pl.multiple_of(index * tile, tile), tile)
            spread = lax.dot_general(
                pair[:, :count * node_cell], picks[rows, group], NT,
                preferred_element_type=jnp.float32,
            )
            totals[:, rows] += spread[:states] + spread[states:]
            return carry

        lax.fori_loop(0, extent // tile, scatter_tile, 0)

    extended[:, :nodes] = f_ref[...]
    pl.semaphore_wait(barrier, 2)

    def one_step(step, carry):
        edge_out[step] = jnp.dot(
            extended[:, :nodes], surface_pick[...], preferred_element_type=jnp.float32
        ).astype(jnp.bfloat16)
        edge = pltpu.make_async_remote_copy(
            src_ref=edge_out.at[step], dst_ref=edge_in.at[step],
            send_sem=edge_send.at[step], recv_sem=edge_recv.at[step],
            device_id={"dom": before}, device_id_type=MESH,
        )
        edge.start()
        totals[...] = jnp.zeros_like(totals)
        run_cells(0, inner // 2, nodes)
        edge.wait()
        ghosts = edge_in[step]
        extended[:, nodes:] = jnp.where(me == n_dom - 1, jnp.zeros_like(ghosts), ghosts)
        run_cells(inner, cells, width)
        back_out[step] = totals[:, nodes:]
        back = pltpu.make_async_remote_copy(
            src_ref=back_out.at[step], dst_ref=back_in.at[step],
            send_sem=back_send.at[step], recv_sem=back_recv.at[step],
            device_id={"dom": after}, device_id_type=MESH,
        )
        back.start()
        run_cells(inner // 2, inner, nodes)
        back.wait()
        returned = back_in[step]
        returned = jnp.where(me == 0, jnp.zeros_like(returned), returned)
        parts = halves(returned)
        first = step == 0
        for start in range(0, nodes, tile):
            columns = pl.ds(start, tile)
            spread = lax.dot_general(
                parts, surface_pick[columns, :], NT, preferred_element_type=jnp.float32
            )
            total = totals[:, columns] + (spread[:states] + spread[states:])
            old = extended[:, columns]
            newest = old.astype(jnp.float32)
            image = total + potential_ref[:, columns] * newest
            shifted = (image - center * newest) / half_width
            later = 2.0 * shifted - history[:, columns].astype(jnp.float32)
            fresh = jnp.where(first, shifted, later).astype(jnp.bfloat16)
            history[:, columns] = old
            extended[:, columns] = fresh
        return carry

    history[...] = jnp.zeros_like(history)
    lax.fori_loop(0, DEGREE, one_step, 0)
    out_ref[...] = extended[:, :nodes]


def filtered_states(orbitals, cell_matrix, connectivity, surface_nodes, cell_scale, potential):
    states, nodes = orbitals.shape
    cells, node_cell = connectivity.shape
    surf = surface_nodes.shape[1]
    vmem = pl.BlockSpec(memory_space=pltpu.VMEM)
    smem = pl.BlockSpec(memory_space=pltpu.SMEM)
    bf16, f32 = jnp.bfloat16, jnp.float32
    return pl.pallas_call(
        functools.partial(filter_kernel, lax.axis_size("dom"), cells - cells // 4),
        out_shape=jax.ShapeDtypeStruct((states, nodes), bf16),
        in_specs=[vmem, vmem, vmem, vmem, smem, vmem],
        out_specs=vmem,
        scratch_shapes=[
            pltpu.VMEM((states, nodes + surf), bf16),
            pltpu.VMEM((states, nodes), bf16),
            pltpu.VMEM((states, nodes + surf), f32),
            pltpu.VMEM((nodes + surf, cells * node_cell), bf16),
            pltpu.VMEM((nodes, surf), bf16),
            pltpu.VMEM((2 * states, cells * node_cell), bf16),
            pltpu.VMEM((DEGREE, states, surf), bf16),
            pltpu.VMEM((DEGREE, states, surf), bf16),
            pltpu.VMEM((DEGREE, states, surf), f32),
            pltpu.VMEM((DEGREE, states, surf), f32),
        ] + [pltpu.SemaphoreType.DMA((DEGREE,))] * 4,
        compiler_params=pltpu.CompilerParams(
            collective_id=0, has_side_effects=True, vmem_limit_bytes=52 * 1024 * 1024
        ),
        name="chebyshev_filter",
    )(orbitals, cell_matrix, connectivity, surface_nodes, cell_scale, potential[None, :])


def product(left, right):
    left_high = left.astype(jnp.bfloat16)
    left_low = (left - left_high.astype(jnp.float32)).astype(jnp.bfloat16)
    right_high = right.astype(jnp.bfloat16)
    right_low = (right - right_high.astype(jnp.float32)).astype(jnp.bfloat16)
    dot = functools.partial(jnp.dot, preferred_element_type=jnp.float32)
    return dot(left_high, right_high) + (dot(left_high, right_low) + dot(left_low, right_high))


def tail_kernel(
    n_dom, n_st, node_total,
    f_ref, out_ref,
    slabs, gram_out, gram_in, chunk_out, chunk_in, gathered, gram_ref, growing_ref, inverse_ref,
    rotation_ref, rotated, *sems,
):
    (slab_send, slab_recv, gram_send, gram_recv, chunk_send, chunk_recv,
     dom_send, dom_recv, st_send, st_recv, out_send, out_recv) = sems
    states, nodes = f_ref.shape
    part = nodes // n_st
    rows = states // n_dom
    states_all = states * n_st
    d, q = lax.axis_index("dom"), lax.axis_index("st")

    def peer(k):
        return lax.rem(q + k, n_st)

    def along(j):
        return lax.rem(d + j, n_dom)

    barrier = pltpu.get_barrier_semaphore()
    for k in range(1, n_st):
        pl.semaphore_signal(barrier, inc=1, device_id={"st": peer(k)}, device_id_type=MESH)
    for j in range(1, n_dom):
        pl.semaphore_signal(barrier, inc=1, device_id={"dom": along(j)}, device_id_type=MESH)
    pl.semaphore_wait(barrier, n_st + n_dom - 2)

    def send(src, dst, send_sem, recv_sem, target):
        copy = pltpu.make_async_remote_copy(
            src_ref=src, dst_ref=dst, send_sem=send_sem, recv_sem=recv_sem,
            device_id=target, device_id_type=MESH,
        )
        copy.start()
        return copy

    def columns(p):
        return pl.ds(pl.multiple_of(p * part, part), part)

    def band(p):
        return pl.ds(pl.multiple_of(p * states, states), states)

    sent = []
    slab = [
        send(f_ref.at[:, columns(peer(k))], slabs.at[band(q), :],
             slab_send.at[k], slab_recv.at[k], {"st": peer(k)})
        for k in range(1, n_st)
    ]
    slabs[band(q), :] = f_ref[:, columns(q)]
    for copy in slab:
        copy.wait()

    def gram_rows(p):
        return lax.dot_general(slabs[band(p), :], slabs[...], NT, preferred_element_type=jnp.float32)

    grams = []
    for k in range(1, n_st):
        gram_out[k] = gram_rows(peer(k))
        grams.append(send(gram_out.at[k], gram_in.at[k], gram_send.at[k], gram_recv.at[k],
                          {"st": peer(k)}))
    total = gram_rows(q)
    for k in range(1, n_st):
        grams[k - 1].wait()
        total += gram_in[k]
    for j in range(n_dom):
        chunk_out[j] = total[j * rows:(j + 1) * rows]
    chunks = [
        send(chunk_out.at[along(j)], chunk_in.at[j], chunk_send.at[j], chunk_recv.at[j],
             {"dom": along(j)})
        for j in range(1, n_dom)
    ]
    mine = chunk_out[d]
    for j in range(1, n_dom):
        chunks[j - 1].wait()
        mine += chunk_in[j]
    gathered[q, d] = mine

    def spread(source, slot):
        return [
            send(gathered.at[q, source], gathered.at[q, source],
                 st_send.at[k, slot], st_recv.at[k, slot], {"st": peer(k)})
            for k in range(1, n_st)
        ]

    doms = [
        send(gathered.at[q, d], gathered.at[q, d], dom_send.at[j], dom_recv.at[j],
             {"dom": along(j)})
        for j in range(1, n_dom)
    ]
    sent = spread(d, 0)
    for j in range(1, n_dom):
        doms[j - 1].wait_recv()
        sent += spread(lax.rem(d + n_dom - j, n_dom), j)
    for copy in doms:
        copy.wait_send()
    for copy in sent:
        copy.wait()
    for p in range(n_st):
        for j in range(n_dom):
            start = p * states + j * rows
            gram_ref[start:start + rows, :] = gathered[p, j]

    gram = gram_ref[...]
    scale_sum = jnp.sqrt(jnp.sum(gram * gram, keepdims=True)) + epsilon
    shape = (states_all, states_all)
    identity = jnp.where(
        lax.broadcasted_iota(jnp.int32, shape, 0) == lax.broadcasted_iota(jnp.int32, shape, 1),
        1.0, 0.0,
    )
    growing_ref[...] = gram / scale_sum
    for iteration in range(ROOT_ITERS):
        if iteration == 0:
            factor = 1.5 * identity - 0.5 * growing_ref[...]
            inverse = factor
        else:
            factor = 1.5 * identity - 0.5 * product(inverse_ref[...], growing_ref[...])
            inverse = product(factor, inverse_ref[...])
        if iteration < ROOT_ITERS - 1:
            growing_ref[...] = product(growing_ref[...], factor)
        inverse_ref[...] = inverse
    rotation_ref[...] = jnp.transpose(
        inverse_ref[...] * jnp.sqrt(node_total / scale_sum)
    ).astype(jnp.bfloat16)

    def rotate(p):
        return jnp.dot(
            rotation_ref[band(p), :], slabs[...], preferred_element_type=jnp.float32
        ).astype(jnp.bfloat16)

    outs = []
    for k in range(1, n_st):
        rotated[k] = rotate(peer(k))
        outs.append(send(rotated.at[k], out_ref.at[:, columns(q)], out_send.at[k], out_recv.at[k],
                         {"st": peer(k)}))
    out_ref[:, columns(q)] = rotate(q)
    for copy in outs:
        copy.wait()


def tail_in_kernel(newest):
    n_dom, n_st = lax.axis_size("dom"), lax.axis_size("st")
    states, nodes = newest.shape
    part, rows, states_all = nodes // n_st, states // n_dom, states * n_st
    vmem = pl.BlockSpec(memory_space=pltpu.VMEM)
    bf16, f32 = jnp.bfloat16, jnp.float32
    square = pltpu.VMEM((states_all, states_all), f32)
    return pl.pallas_call(
        functools.partial(tail_kernel, n_dom, n_st, float(n_dom * nodes)),
        out_shape=jax.ShapeDtypeStruct((states, nodes), bf16),
        in_specs=[vmem],
        out_specs=vmem,
        scratch_shapes=[
            pltpu.VMEM((states_all, part), bf16),
            pltpu.VMEM((n_st, states, states_all), f32),
            pltpu.VMEM((n_st, states, states_all), f32),
            pltpu.VMEM((n_dom, rows, states_all), f32),
            pltpu.VMEM((n_dom, rows, states_all), f32),
            pltpu.VMEM((n_st, n_dom, rows, states_all), f32),
            square, square, square,
            pltpu.VMEM((states_all, states_all), bf16),
            pltpu.VMEM((n_st, states, part), bf16),
        ] + [pltpu.SemaphoreType.DMA((n_st,))] * 4
        + [pltpu.SemaphoreType.DMA((n_dom,))] * 4
        + [pltpu.SemaphoreType.DMA((n_st, n_dom))] * 2
        + [pltpu.SemaphoreType.DMA((n_st,))] * 2,
        compiler_params=pltpu.CompilerParams(
            collective_id=1, has_side_effects=True, vmem_limit_bytes=40 * 1024 * 1024
        ),
        name="gram_and_rotation",
    )(newest)


def newton_root(gram):
    highest = lax.Precision.HIGHEST
    states_all = gram.shape[0]
    scale_sum = jnp.sqrt(jnp.sum(gram * gram)) + epsilon
    identity = jnp.eye(states_all, dtype=jnp.float32)
    growing = gram / scale_sum
    inverse = identity
    for iteration in range(ROOT_ITERS):
        factor = 1.5 * identity - 0.5 * jnp.dot(inverse, growing, precision=highest)
        growing = jnp.dot(growing, factor, precision=highest)
        inverse = jnp.dot(factor, inverse, precision=highest)
    return (inverse, scale_sum)


def tail_in_parts(newest):
    slabs = lax.all_to_all(newest, "st", split_axis=1, concat_axis=0, tiled=True)
    gram_part = jnp.dot(slabs, slabs.T, preferred_element_type=jnp.float32)
    row_block = lax.psum_scatter(gram_part, "st", scatter_dimension=0, tiled=True)
    row_block = lax.psum(row_block, "dom")
    gram = lax.all_gather(row_block, "st", axis=0, tiled=True)
    inverse, scale_sum = newton_root(gram)
    node_total = lax.axis_size("dom") * newest.shape[1]
    rotation = (inverse * jnp.sqrt(node_total / scale_sum)).astype(jnp.bfloat16)
    rotated = jnp.dot(rotation.T, slabs, preferred_element_type=jnp.float32).astype(jnp.bfloat16)
    return lax.all_to_all(rotated, "st", split_axis=0, concat_axis=1, tiled=True)


def body(orbitals, cell_matrix, connectivity, surface_nodes, cell_scale, potential):
    newest = filtered_states(
        orbitals, cell_matrix, connectivity, surface_nodes, cell_scale, potential
    )
    if orbitals.shape[0] % lax.axis_size("dom") == 0:
        return tail_in_kernel(newest)
    return tail_in_parts(newest)


def solution(mesh):
    return jax.shard_map(
        body,
        mesh=mesh,
        in_specs=(P("st", "dom"), P(), P("dom", None), P("dom", None), P("dom"), P("dom")),
        out_specs=P("st", "dom"),
        check_vma=False,
    )
```

time: 221 us -> 132 us (0.60)
  waiting for transfers between devices: 77.8 us -> 0 us
  Pallas kernels: 78.1 us -> 127 us
  blocking collectives: 29.7 us -> 0 us
  matrix products: 14.4 us -> 0 us
  between operations: 14.3 us -> 0.02 us
    psum x1 -> x0, waiting for transfers between devices: 54.5 us -> none  [body(): row_block = lax.psum(row_block, 'dom')]
    pallas_call x0 -> x1, Pallas kernels: none -> 52 us  [tail_in_kernel(): pl.pallas_call(functools.partial(tail_kernel, n_dom, n_st, float(n_dom *...]
    reduce_scatter x1 -> x0, waiting for transfers between devices: 23.3 us -> none  [body(): lax.psum_scatter(gram_part, 'st', scatter_dimension=0, tiled=True)]
    all_to_all x2 -> x0, blocking collectives: 18.9 us -> none  [the longest x1 9.94 us: body(): lax.all_to_all(newest, 'st', split_axis=1, concat_axis=0, tiled=True)]
    dot_general x13 -> x0, matrix products: 14.4 us -> none  [the longest x4 4.58 us: newton_root(): factor = 1.5 * identity - 0.5 * jnp.dot(inverse, growing, precision=highest)]
    all_gather x1 -> x0, blocking collectives: 10.8 us -> none  [body(): gram = lax.all_gather(row_block, 'st', axis=0, tiled=True)]
    pallas_call x1, Pallas kernels: 78.1 us -> 74.7 us  [filtered_states(): pl.pallas_call(functools.partial(filter_kernel, lax.axis_size('dom'), cel...]
    unnamed x12 -> x13, local copies, waits for them, and re-layouts: 4.18 us -> 4.93 us
  transfers between devices with their start and end apart: 2 -> 0, of which waited for: 2 -> 0; matrix products, arithmetic and copies ran while one was open for 0% -> 0% of each run, Pallas kernels for 0% -> 0%
where the time goes in v2:
time: 132 us
  Pallas kernels  127 us (96%)
  local copies, waits for them, and re-layouts  4.93 us (4%)
    pallas_call x1, Pallas kernels, filtered_states(): pl.pallas_call(functools.partial(filter_kernel, lax.axis_size('dom'), cel...  74.7 us
    pallas_call x1, Pallas kernels, tail_in_kernel(): pl.pallas_call(functools.partial(tail_kernel, n_dom, n_st, float(n_dom *...  52 us
    unnamed x13, local copies, waits for them, and re-layouts  4.93 us

profile of v2, /device:TPU:0, one launch (start us, length us, event | category | flops | bytes accessed | tf_op | source)
XLA Modules:
  0.0 131.7 jit_solution(3016581554002293984)
XLA Ops:
  0.0 0.0 copy-start.5
  0.0 0.0 copy-start.4
  0.0 0.7 copy-done.5
  0.7 0.0 copy-done.4
  0.7 0.0 copy-start
  0.7 1.0 copy-done
  1.7 0.0 copy-start.1
  1.7 1.0 copy-done.1
  2.7 0.0 copy-start.2
  2.7 0.8 copy-done.2
  3.5 0.0 copy-start.3
  3.5 0.7 copy-done.3
  4.2 74.7 %chebyshev_filter.1.f_ref = bf16[96,2048]{1,0:T(8,128)(2,1)S(1)} custom-call(bf16[96,2048]{1,0:T(8,128)(2,1)S(1)} %copy-done.1, bf16[512,512]{1,0:T(8,128)(2,1)S(1)} %copy-done, s32[16,512]{1,0:T(8,128)S(1)} %copy-done.2, s32[1,256]{1,0:T(1,128)S(1)} %copy-done.4, f32[16]{0:T(128)S(1)} %copy-done.5, f32[1,2048]{1,0:T(1,128)S(1)} %bitcast.1), custom_call_target="tpu_custom_call" | custom-call | tf_op jit(solution)/shard_map/chebyshev_filter/pallas_call | solution.py:152
  78.9 52.0 %gram_and_rotation.1 = bf16[96,2048]{1,0:T(8,128)(2,1)S(1)} custom-call(bf16[96,2048]{1,0:T(8,128)(2,1)S(1)} %chebyshev_filter.1.f_ref), custom_call_target="tpu_custom_call" | custom-call | tf_op jit(solution)/shard_map/gram_and_rotation/pallas_call | solution.py:330
  130.9 0.7 copy.8
Async XLA Ops:
  0.0 0.7 copy-start.5
  0.0 0.7 copy-start.4
  0.7 1.0 copy-start
  1.7 1.0 copy-start.1
  2.7 0.8 copy-start.2
  3.5 0.7 copy-start.3

commit v3 on v2

--- a/solution.py
+++ b/solution.py
@@ -26,11 +26,11 @@
 
 def filter_kernel(
     n_dom, inner,
-    f_ref, matrix_ref, conn_ref, surface_ref, scale_ref, potential_ref, out_ref,
-    extended, history, totals, picks, surface_pick, pair, edge_out, edge_in, back_out, back_in,
-    edge_send, edge_recv, back_send, back_recv,
+    f_hbm, matrix_hbm, conn_hbm, surface_hbm, scale_ref, potential_hbm, out_ref,
+    matrix_ref, conn_ref, surface_ref, potential_ref, extended, history, totals, picks, surface_pick, pair, edge_out, edge_in, back_out, back_in,
+    edge_send, edge_recv, back_send, back_recv, load_sems,
 ):
-    states, nodes = f_ref.shape
+    states, nodes = f_hbm.shape
     surf = surface_ref.shape[1]
     cells, node_cell = conn_ref.shape
     width = nodes + surf
@@ -42,6 +42,17 @@
     for neighbour in (after, before):
         pl.semaphore_signal(barrier, inc=1, device_id={"dom": neighbour}, device_id_type=MESH)
 
+    loads = [
+        pltpu.make_async_copy(src, dst, load_sems.at[index])
+        for index, (src, dst) in enumerate([
+            (conn_hbm, conn_ref), (surface_hbm, surface_ref),
+            (f_hbm, extended.at[:, pl.ds(0, nodes)]), (matrix_hbm, matrix_ref),
+            (potential_hbm, potential_ref),
+        ])
+    ]
+    for load in loads:
+        load.start()
+
     def one_hot(ids, start):
         columns = ids.shape[1]
         node = lax.broadcasted_iota(jnp.int32, (tile, columns), 0).astype(jnp.bfloat16)
@@ -49,27 +60,39 @@
         one, zero = jnp.bfloat16(1), jnp.bfloat16(0)
         return jnp.where(node == wanted, one, zero)
 
+    loads[0].wait()
+    ids_down = jnp.transpose(conn_ref[...].astype(jnp.float32))
+    for cell in range(cells):
+        wanted = jnp.broadcast_to(ids_down[:, cell:cell + 1], (node_cell, tile))
+        lanes = lax.broadcasted_iota(jnp.int32, (node_cell, tile), 1).astype(jnp.bfloat16)
+        rows = pl.ds(cell * node_cell, node_cell)
+
+        def build_tile(index, carry):
+            start = index * tile
+            shifted = (wanted - start.astype(jnp.float32)).astype(jnp.bfloat16)
+            picks[rows, pl.ds(pl.multiple_of(start, tile), tile)] = jnp.where(
+                lanes == shifted, jnp.bfloat16(1), jnp.bfloat16(0)
+            )
+            return carry
+
+        lax.fori_loop(0, (nodes if cell < inner else width) // tile, build_tile, 0)
+    for load in loads[1:]:
+        load.wait()
     for start in range(0, nodes, tile):
         surface_pick[pl.ds(start, tile), :] = one_hot(surface_ref[...], start)
-    for cell in range(cells):
-        ids = conn_ref[pl.ds(cell, 1), :]
-        lanes = pl.ds(cell * node_cell, node_cell)
-
-        def build_tile(index, carry):
-            start = index * tile
-            picks[pl.ds(pl.multiple_of(start, tile), tile), lanes] = one_hot(ids, start)
-            return carry
-
-        lax.fori_loop(0, (nodes if cell < inner else width) // tile, build_tile, 0)
 
     def run_cells(first, last, extent):
         count = last - first
         gathered = []
         for cell in range(first, last):
-            lanes = pl.ds(cell * node_cell, node_cell)
-            gathered.append(jnp.dot(
-                extended[:, :extent], picks[:extent, lanes], preferred_element_type=jnp.float32
-            ).astype(jnp.bfloat16))
+            ids = conn_ref[pl.ds(cell, 1), :]
+            found = jnp.zeros((states, node_cell), jnp.float32)
+            for start in range(0, extent, tile):
+                found += jnp.dot(
+                    extended[:, start:start + tile], one_hot(ids, start),
+                    preferred_element_type=jnp.float32,
+                )
+            gathered.append(found.astype(jnp.bfloat16))
         products = jnp.dot(
             jnp.concatenate(gathered, axis=0), matrix_ref[...], preferred_element_type=jnp.float32
         )
@@ -79,17 +102,16 @@
         group = pl.ds(first * node_cell, count * node_cell)
 
         def scatter_tile(index, carry):
-            rows = pl.ds(pl.multiple_of(index * tile, tile), tile)
-            spread = lax.dot_general(
-                pair[:, :count * node_cell], picks[rows, group], NT,
+            columns = pl.ds(pl.multiple_of(index * tile, tile), tile)
+            spread = jnp.dot(
+                pair[:, :count * node_cell], picks[group, columns],
                 preferred_element_type=jnp.float32,
             )
-            totals[:, rows] += spread[:states] + spread[states:]
+            totals[:, columns] += spread[:states] + spread[states:]
             return carry
 
         lax.fori_loop(0, extent // tile, scatter_tile, 0)
 
-    extended[:, :nodes] = f_ref[...]
     pl.semaphore_wait(barrier, 2)
 
     def one_step(step, carry):
@@ -148,24 +170,29 @@
     surf = surface_nodes.shape[1]
     vmem = pl.BlockSpec(memory_space=pltpu.VMEM)
     smem = pl.BlockSpec(memory_space=pltpu.SMEM)
+    hbm = pl.BlockSpec(memory_space=pl.ANY)
     bf16, f32 = jnp.bfloat16, jnp.float32
     return pl.pallas_call(
         functools.partial(filter_kernel, lax.axis_size("dom"), cells - cells // 4),
         out_shape=jax.ShapeDtypeStruct((states, nodes), bf16),
-        in_specs=[vmem, vmem, vmem, vmem, smem, vmem],
+        in_specs=[hbm, hbm, hbm, hbm, smem, hbm],
         out_specs=vmem,
         scratch_shapes=[
+            pltpu.VMEM((node_cell, node_cell), bf16),
+            pltpu.VMEM((cells, node_cell), jnp.int32),
+            pltpu.VMEM((1, surf), jnp.int32),
+            pltpu.VMEM((1, nodes), f32),
             pltpu.VMEM((states, nodes + surf), bf16),
             pltpu.VMEM((states, nodes), bf16),
             pltpu.VMEM((states, nodes + surf), f32),
-            pltpu.VMEM((nodes + surf, cells * node_cell), bf16),
+            pltpu.VMEM((cells * node_cell, nodes + surf), bf16),
             pltpu.VMEM((nodes, surf), bf16),
             pltpu.VMEM((2 * states, cells * node_cell), bf16),
             pltpu.VMEM((DEGREE, states, surf), bf16),
             pltpu.VMEM((DEGREE, states, surf), bf16),
             pltpu.VMEM((DEGREE, states, surf), f32),
             pltpu.VMEM((DEGREE, states, surf), f32),
-        ] + [pltpu.SemaphoreType.DMA((DEGREE,))] * 4,
+        ] + [pltpu.SemaphoreType.DMA((DEGREE,))] * 4 + [pltpu.SemaphoreType.DMA((5,))],
         compiler_params=pltpu.CompilerParams(
             collective_id=0, has_side_effects=True, vmem_limit_bytes=52 * 1024 * 1024
         ),

time: 132 us -> 125 us (0.947)
  Pallas kernels: 127 us -> 120 us
    pallas_call x1, Pallas kernels: 74.7 us -> 67.9 us  [filtered_states(): pl.pallas_call(functools.partial(filter_kernel, lax.axis_size('dom'), cel...]
where the time goes in v3:
time: 125 us
  Pallas kernels  120 us (96%)
  local copies, waits for them, and re-layouts  4.93 us (4%)
    pallas_call x1, Pallas kernels, filtered_states(): pl.pallas_call(functools.partial(filter_kernel, lax.axis_size('dom'), cel...  67.9 us
    pallas_call x1, Pallas kernels, tail_in_kernel(): pl.pallas_call(functools.partial(tail_kernel, n_dom, n_st, float(n_dom *...  51.7 us
    unnamed x13, local copies, waits for them, and re-layouts  4.93 us

profile of v3, /device:TPU:0, one launch (start us, length us, event | category | flops | bytes accessed | tf_op | source)
XLA Modules:
  0.0 124.5 jit_solution(13305041053060704086)
XLA Ops:
  0.0 0.0 copy-start.5
  0.0 0.0 copy-start.4
  0.0 0.7 copy-done.5
  0.7 0.0 copy-done.4
  0.7 0.0 copy-start
  0.7 1.0 copy-done
  1.7 0.0 copy-start.1
  1.7 1.0 copy-done.1
  2.7 0.0 copy-start.2
  2.7 0.8 copy-done.2
  3.5 0.0 copy-start.3
  3.5 0.7 copy-done.3
  4.2 67.9 %chebyshev_filter.1.f_ref = bf16[96,2048]{1,0:T(8,128)(2,1)S(1)} custom-call(bf16[96,2048]{1,0:T(8,128)(2,1)S(1)} %copy-done.1, bf16[512,512]{1,0:T(8,128)(2,1)S(1)} %copy-done, s32[16,512]{1,0:T(8,128)S(1)} %copy-done.2, s32[1,256]{1,0:T(1,128)S(1)} %copy-done.4, f32[16]{0:T(128)S(1)} %copy-done.5, f32[1,2048]{1,0:T(1,128)S(1)} %bitcast.1), custom_call_target="tpu_custom_call" | custom-call | tf_op jit(solution)/shard_map/chebyshev_filter/pallas_call | solution.py:175
  72.1 51.7 %gram_and_rotation.1 = bf16[96,2048]{1,0:T(8,128)(2,1)S(1)} custom-call(bf16[96,2048]{1,0:T(8,128)(2,1)S(1)} %chebyshev_filter.1.f_ref), custom_call_target="tpu_custom_call" | custom-call | tf_op jit(solution)/shard_map/gram_and_rotation/pallas_call | solution.py:357
  123.8 0.7 copy.8
Async XLA Ops:
  0.0 0.7 copy-start.5
  0.0 0.7 copy-start.4
  0.7 1.0 copy-start
  1.7 1.0 copy-start.1
  2.7 0.8 copy-start.2
  3.5 0.7 copy-start.3

commit v4 on v3

v4 whole, which is shorter than its diff:
```python
import functools

import jax
import jax.numpy as jnp
from jax import lax
from jax.experimental import pallas as pl
from jax.experimental.pallas import tpu as pltpu
from jax.sharding import PartitionSpec as P

DEGREE = 3
ROOT_ITERS = 4
MESH = pl.DeviceIdType.MESH

center = 7.0
half_width = 6.0
epsilon = 1e-06

NT = (((1,), (1,)), ((), ()))


def halves(values):
    high = values.astype(jnp.bfloat16)
    low = (values - high.astype(jnp.float32)).astype(jnp.bfloat16)
    return jnp.concatenate([high, low], axis=0)


def greet(n_dom, n_st, everyone):
    d, q = lax.axis_index("dom"), lax.axis_index("st")
    barrier = pltpu.get_barrier_semaphore()
    steps = range(1, n_dom) if everyone else (1, n_dom - 1)
    for j in steps:
        pl.semaphore_signal(
            barrier, inc=1, device_id={"dom": lax.rem(d + j, n_dom)}, device_id_type=MESH
        )
    if everyone:
        for k in range(1, n_st):
            pl.semaphore_signal(
                barrier, inc=1, device_id={"st": lax.rem(q + k, n_st)}, device_id_type=MESH
            )
    return barrier, len(steps) + (n_st - 1 if everyone else 0)


def kernel(
    n_dom, n_st, inner, with_tail,
    f_hbm, matrix_hbm, conn_hbm, surface_hbm, scale_ref, potential_hbm, out_ref,
    matrix_ref, conn_ref, surface_ref, potential_ref, extended, history, totals, picks, surface_pick, pair, edge_out, edge_in, back_out, back_in,
    edge_send, edge_recv, back_send, back_recv, load_sems, *tail_refs,
):
    states, nodes = f_hbm.shape
    surf = surface_ref.shape[1]
    cells, node_cell = conn_ref.shape
    width = nodes + surf
    tile = 256
    me = lax.axis_index("dom")
    after, before = lax.rem(me + 1, n_dom), lax.rem(me + n_dom - 1, n_dom)

    barrier, greetings = greet(n_dom, n_st, with_tail)
    loads = [
        pltpu.make_async_copy(src, dst, load_sems.at[index])
        for index, (src, dst) in enumerate([
            (conn_hbm, conn_ref), (surface_hbm, surface_ref),
            (f_hbm, extended.at[:, pl.ds(0, nodes)]), (matrix_hbm, matrix_ref),
            (potential_hbm, potential_ref),
        ])
    ]
    for load in loads:
        load.start()

    def one_hot(ids, start):
        columns = ids.shape[1]
        node = lax.broadcasted_iota(jnp.int32, (tile, columns), 0).astype(jnp.bfloat16)
        wanted = jnp.broadcast_to((ids - start).astype(jnp.bfloat16), (tile, columns))
        one, zero = jnp.bfloat16(1), jnp.bfloat16(0)
        return jnp.where(node == wanted, one, zero)

    loads[0].wait()
    ids_down = jnp.transpose(conn_ref[...].astype(jnp.float32))
    for cell in range(cells):
        wanted = jnp.broadcast_to(ids_down[:, cell:cell + 1], (node_cell, tile))
        lanes = lax.broadcasted_iota(jnp.int32, (node_cell, tile), 1).astype(jnp.bfloat16)
        rows = pl.ds(cell * node_cell, node_cell)

        def build_tile(index, carry):
            start = index * tile
            shifted = (wanted - start.astype(jnp.float32)).astype(jnp.bfloat16)
            picks[rows, pl.ds(pl.multiple_of(start, tile), tile)] = jnp.where(
                lanes == shifted, jnp.bfloat16(1), jnp.bfloat16(0)
            )
            return carry

        lax.fori_loop(0, (nodes if cell < inner else width) // tile, build_tile, 0)
    for load in loads[1:]:
        load.wait()
    for start in range(0, nodes, tile):
        surface_pick[pl.ds(start, tile), :] = one_hot(surface_ref[...], start)

    def run_cells(first, last, extent):
        count = last - first
        gathered = []
        for cell in range(first, last):
            ids = conn_ref[pl.ds(cell, 1), :]
            found = jnp.zeros((states, node_cell), jnp.float32)
            for start in range(0, extent, tile):
                found += jnp.dot(
                    extended[:, start:start + tile], one_hot(ids, start),
                    preferred_element_type=jnp.float32,
                )
            gathered.append(found.astype(jnp.bfloat16))
        products = jnp.dot(
            jnp.concatenate(gathered, axis=0), matrix_ref[...], preferred_element_type=jnp.float32
        )
        for index in range(count):
            scaled = products[index * states:(index + 1) * states] * scale_ref[first + index]
            pair[:, index * node_cell:(index + 1) * node_cell] = halves(scaled)
        group = pl.ds(first * node_cell, count * node_cell)

        for start in range(0, extent, tile):
            columns = pl.ds(start, tile)
            spread = jnp.dot(
                pair[:, :count * node_cell], picks[group, columns],
                preferred_element_type=jnp.float32,
            )
            totals[:, columns] += spread[:states] + spread[states:]

    pl.semaphore_wait(barrier, greetings)

    def one_step(step, carry):
        edge_out[step] = jnp.dot(
            extended[:, :nodes], surface_pick[...], preferred_element_type=jnp.float32
        ).astype(jnp.bfloat16)
        edge = pltpu.make_async_remote_copy(
            src_ref=edge_out.at[step], dst_ref=edge_in.at[step],
            send_sem=edge_send.at[step], recv_sem=edge_recv.at[step],
            device_id={"dom": before}, device_id_type=MESH,
        )
        edge.start()
        totals[...] = jnp.zeros_like(totals)
        run_cells(0, inner // 2, nodes)
        edge.wait()
        ghosts = edge_in[step]
        extended[:, nodes:] = jnp.where(me == n_dom - 1, jnp.zeros_like(ghosts), ghosts)
        run_cells(inner, cells, width)
        back_out[step] = totals[:, nodes:]
        back = pltpu.make_async_remote_copy(
            src_ref=back_out.at[step], dst_ref=back_in.at[step],
            send_sem=back_send.at[step], recv_sem=back_recv.at[step],
            device_id={"dom": after}, device_id_type=MESH,
        )
        back.start()
        run_cells(inner // 2, inner, nodes)
        back.wait()
        returned = back_in[step]
        returned = jnp.where(me == 0, jnp.zeros_like(returned), returned)
        parts = halves(returned)
        first = step == 0
        for start in range(0, nodes, tile):
            columns = pl.ds(start, tile)
            spread = lax.dot_general(
                parts, surface_pick[columns, :], NT, preferred_element_type=jnp.float32
            )
            total = totals[:, columns] + (spread[:states] + spread[states:])
            old = extended[:, columns]
            newest = old.astype(jnp.float32)
            image = total + potential_ref[:, columns] * newest
            shifted = (image - center * newest) / half_width
            later = 2.0 * shifted - history[:, columns].astype(jnp.float32)
            fresh = jnp.where(first, shifted, later).astype(jnp.bfloat16)
            history[:, columns] = old
            extended[:, columns] = fresh
        return carry

    history[...] = jnp.zeros_like(history)
    lax.fori_loop(0, DEGREE, one_step, 0)
    if with_tail:
        tail_part(n_dom, n_st, float(n_dom * nodes), states, nodes, extended, out_ref, *tail_refs)
    else:
        out_ref[...] = extended[:, :nodes]


def product(left, right):
    left_high = left.astype(jnp.bfloat16)
    left_low = (left - left_high.astype(jnp.float32)).astype(jnp.bfloat16)
    right_high = right.astype(jnp.bfloat16)
    right_low = (right - right_high.astype(jnp.float32)).astype(jnp.bfloat16)
    dot = functools.partial(jnp.dot, preferred_element_type=jnp.float32)
    return dot(left_high, right_high) + (dot(left_high, right_low) + dot(left_low, right_high))


def tail_part(
    n_dom, n_st, node_total, states, nodes,
    f_ref, out_ref,
    full, gram_out, gram_in, chunk_out, chunk_in, gathered, gram_ref, growing_ref, inverse_ref,
    *sems,
):
    (slab_send, slab_recv, gram_send, gram_recv, chunk_send, chunk_recv,
     dom_send, dom_recv, st_send, st_recv, rest_send, rest_recv) = sems
    part = nodes // n_st
    rows = states // n_dom
    states_all = states * n_st
    d, q = lax.axis_index("dom"), lax.axis_index("st")

    def peer(k):
        return lax.rem(q + k, n_st)

    def along(j):
        return lax.rem(d + j, n_dom)

    def send(src, dst, send_sem, recv_sem, target):
        copy = pltpu.make_async_remote_copy(
            src_ref=src, dst_ref=dst, send_sem=send_sem, recv_sem=recv_sem,
            device_id=target, device_id_type=MESH,
        )
        copy.start()
        return copy

    def columns(p):
        return pl.ds(pl.multiple_of(p * part, part), part)

    def band(p):
        return pl.ds(pl.multiple_of(p * states, states), states)

    slab = [
        send(f_ref.at[:, columns(peer(k))], full.at[band(q), columns(peer(k))],
             slab_send.at[k], slab_recv.at[k], {"st": peer(k)})
        for k in range(1, n_st)
    ]

    def send_rest(m):
        return [
            send(f_ref.at[:, columns(peer(k + m))], full.at[band(q), columns(peer(k + m))],
                 rest_send.at[k, m], rest_recv.at[k, m], {"st": peer(k)})
            for k in range(1, n_st)
        ]

    full[band(q), :] = f_ref[:, :nodes]
    for copy in slab:
        copy.wait()

    def gram_rows(p):
        return lax.dot_general(
            full[band(p), columns(q)], full[:, columns(q)], NT,
            preferred_element_type=jnp.float32,
        )

    grams = []
    for k in range(1, n_st):
        gram_out[k] = gram_rows(peer(k))
        grams.append(send(gram_out.at[k], gram_in.at[k], gram_send.at[k], gram_recv.at[k],
                          {"st": peer(k)}))
    total = gram_rows(q)
    for k in range(1, n_st):
        grams[k - 1].wait()
        total += gram_in[k]
    for j in range(n_dom):
        chunk_out[j] = total[j * rows:(j + 1) * rows]
    chunks = [
        send(chunk_out.at[along(j)], chunk_in.at[j], chunk_send.at[j], chunk_recv.at[j],
             {"dom": along(j)})
        for j in range(1, n_dom)
    ]
    rest = []
    for m in range(1, n_st - 1):
        rest += send_rest(m)
    mine = chunk_out[d]
    for j in range(1, n_dom):
        chunks[j - 1].wait()
        mine += chunk_in[j]
    gathered[q, d] = mine

    def spread(source, slot):
        return [
            send(gathered.at[q, source], gathered.at[q, source],
                 st_send.at[k, slot], st_recv.at[k, slot], {"st": peer(k)})
            for k in range(1, n_st)
        ]

    doms = [
        send(gathered.at[q, d], gathered.at[q, d], dom_send.at[j], dom_recv.at[j],
             {"dom": along(j)})
        for j in range(1, n_dom)
    ]
    sent = spread(d, 0)
    for j in range(1, n_dom):
        doms[j - 1].wait_recv()
        sent += spread(lax.rem(d + n_dom - j, n_dom), j)
    for copy in doms:
        copy.wait_send()
    for copy in sent:
        copy.wait()
    rest += send_rest(n_st - 1)
    for p in range(n_st):
        for j in range(n_dom):
            start = p * states + j * rows
            gram_ref[start:start + rows, :] = gathered[p, j]

    gram = gram_ref[...]
    scale_sum = jnp.sqrt(jnp.sum(gram * gram, keepdims=True)) + epsilon

    def factor_of(product_rows, start):
        shape = product_rows.shape
        row_ids = start + lax.broadcasted_iota(jnp.int32, shape, 0)
        column_ids = lax.broadcasted_iota(jnp.int32, shape, 1)
        return jnp.where(row_ids == column_ids, 1.5, 0.0) - 0.5 * product_rows

    growing_ref[...] = gram / scale_sum
    for iteration in range(ROOT_ITERS - 1):
        if iteration == 0:
            factor = factor_of(growing_ref[...], 0)
            inverse = factor
        else:
            factor = factor_of(product(inverse_ref[...], growing_ref[...]), 0)
            inverse = product(factor, inverse_ref[...])
        growing_ref[...] = product(growing_ref[...], factor)
        inverse_ref[...] = inverse
    factor = factor_of(product(inverse_ref[band(q), :], growing_ref[...]), q * states)
    inverse = product(factor, inverse_ref[...])
    rotation = (inverse * jnp.sqrt(node_total / scale_sum)).astype(jnp.bfloat16)
    for copy in rest:
        copy.wait()
    for start in range(0, nodes, part):
        out_ref[:, start:start + part] = jnp.dot(
            rotation, full[:, start:start + part], preferred_element_type=jnp.float32
        ).astype(jnp.bfloat16)


def run_kernel(
    with_tail, orbitals, cell_matrix, connectivity, surface_nodes, cell_scale, potential
):
    states, nodes = orbitals.shape
    cells, node_cell = connectivity.shape
    surf = surface_nodes.shape[1]
    vmem = pl.BlockSpec(memory_space=pltpu.VMEM)
    smem = pl.BlockSpec(memory_space=pltpu.SMEM)
    hbm = pl.BlockSpec(memory_space=pl.ANY)
    bf16, f32 = jnp.bfloat16, jnp.float32
    n_dom, n_st = lax.axis_size("dom"), lax.axis_size("st")
    tail_scratch = []
    if with_tail:
        rows, states_all = states // n_dom, states * n_st
        square = pltpu.VMEM((states_all, states_all), f32)
        tail_scratch = [
            pltpu.VMEM((states_all, nodes), bf16),
            pltpu.VMEM((n_st, states, states_all), f32),
            pltpu.VMEM((n_st, states, states_all), f32),
            pltpu.VMEM((n_dom, rows, states_all), f32),
            pltpu.VMEM((n_dom, rows, states_all), f32),
            pltpu.VMEM((n_st, n_dom, rows, states_all), f32),
            square, square, square,
        ]
        tail_scratch += [pltpu.SemaphoreType.DMA((n_st,))] * 4
        tail_scratch += [pltpu.SemaphoreType.DMA((n_dom,))] * 4
        tail_scratch += [pltpu.SemaphoreType.DMA((n_st, n_dom))] * 2
        tail_scratch += [pltpu.SemaphoreType.DMA((n_st, n_st))] * 2
    return pl.pallas_call(
        functools.partial(kernel, n_dom, n_st, cells - cells // 4, with_tail),
        out_shape=jax.ShapeDtypeStruct((states, nodes), bf16),
        in_specs=[hbm, hbm, hbm, hbm, smem, hbm],
        out_specs=vmem,
        scratch_shapes=[
            pltpu.VMEM((node_cell, node_cell), bf16),
            pltpu.VMEM((cells, node_cell), jnp.int32),
            pltpu.VMEM((1, surf), jnp.int32),
            pltpu.VMEM((1, nodes), f32),
            pltpu.VMEM((states, nodes + surf), bf16),
            pltpu.VMEM((states, nodes), bf16),
            pltpu.VMEM((states, nodes + surf), f32),
            pltpu.VMEM((cells * node_cell, nodes + surf), bf16),
            pltpu.VMEM((nodes, surf), bf16),
            pltpu.VMEM((2 * states, cells * node_cell), bf16),
            pltpu.VMEM((DEGREE, states, surf), bf16),
            pltpu.VMEM((DEGREE, states, surf), bf16),
            pltpu.VMEM((DEGREE, states, surf), f32),
            pltpu.VMEM((DEGREE, states, surf), f32),
        ] + [pltpu.SemaphoreType.DMA((DEGREE,))] * 4 + [pltpu.SemaphoreType.DMA((5,))]
        + tail_scratch,
        compiler_params=pltpu.CompilerParams(
            collective_id=0, has_side_effects=True, vmem_limit_bytes=60 * 1024 * 1024
        ),
        name="filter_and_rotation" if with_tail else "filter",
    )(orbitals, cell_matrix, connectivity, surface_nodes, cell_scale, potential[None, :])


def newton_root(gram):
    highest = lax.Precision.HIGHEST
    states_all = gram.shape[0]
    scale_sum = jnp.sqrt(jnp.sum(gram * gram)) + epsilon
    identity = jnp.eye(states_all, dtype=jnp.float32)
    growing = gram / scale_sum
    inverse = identity
    for iteration in range(ROOT_ITERS):
        factor = 1.5 * identity - 0.5 * jnp.dot(inverse, growing, precision=highest)
        growing = jnp.dot(growing, factor, precision=highest)
        inverse = jnp.dot(factor, inverse, precision=highest)
    return (inverse, scale_sum)


def tail_in_parts(newest):
    slabs = lax.all_to_all(newest, "st", split_axis=1, concat_axis=0, tiled=True)
    gram_part = jnp.dot(slabs, slabs.T, preferred_element_type=jnp.float32)
    row_block = lax.psum_scatter(gram_part, "st", scatter_dimension=0, tiled=True)
    row_block = lax.psum(row_block, "dom")
    gram = lax.all_gather(row_block, "st", axis=0, tiled=True)
    inverse, scale_sum = newton_root(gram)
    node_total = lax.axis_size("dom") * newest.shape[1]
    rotation = (inverse * jnp.sqrt(node_total / scale_sum)).astype(jnp.bfloat16)
    rotated = jnp.dot(rotation.T, slabs, preferred_element_type=jnp.float32).astype(jnp.bfloat16)
    return lax.all_to_all(rotated, "st", split_axis=0, concat_axis=1, tiled=True)


def body(orbitals, *others):
    if orbitals.shape[0] % lax.axis_size("dom") == 0:
        return run_kernel(True, orbitals, *others)
    return tail_in_parts(run_kernel(False, orbitals, *others))


def solution(mesh):
    return jax.shard_map(
        body,
        mesh=mesh,
        in_specs=(P("st", "dom"), P(), P("dom", None), P("dom", None), P("dom"), P("dom")),
        out_specs=P("st", "dom"),
        check_vma=False,
    )
```

time: 125 us -> 99.7 us (0.80)
  Pallas kernels: 120 us -> 97.7 us
  local copies, waits for them, and re-layouts: 4.93 us -> 1.77 us
    pallas_call x2 -> x1, Pallas kernels: 120 us -> 97.7 us  [run_kernel(): pl.pallas_call(functools.partial(kernel, n_dom, n_st, cells - cells // 4,...]
    unnamed x13 -> x1, local copies, waits for them, and re-layouts: 4.93 us -> 1.77 us
where the time goes in v4:
time: 99.7 us; the launch traced here: 99.5 us
  Pallas kernels  97.7 us (98%)
  local copies, waits for them, and re-layouts  1.77 us (2%)
    pallas_call x1, Pallas kernels, run_kernel(): pl.pallas_call(functools.partial(kernel, n_dom, n_st, cells - cells // 4,...  97.7 us

profile of v4, /device:TPU:0, one launch (start us, length us, event | category | flops | bytes accessed | tf_op | source)
XLA Modules:
  0.0 99.5 jit_solution(8732351786968105601)
XLA Ops:
  0.0 97.7 %filter_and_rotation.1 = bf16[96,2048]{1,0:T(8,128)(2,1)} custom-call(bf16[96,2048]{1,0:T(8,128)(2,1)} %f_hbm.1, bf16[512,512]{1,0:T(8,128)(2,1)} %matrix_hbm.1, s32[16,512]{1,0:T(8,128)} %conn_hbm.1, s32[1,256]{1,0:T(1,128)} %surface_hbm.1, f32[16]{0:T(128)} %scale_ref.1, f32[1,2048]{1,0:T(1,128)} %bitcast.1), custom_call_target="tpu_custom_call" | custom-call | tf_op jit(solution)/shard_map/filter_and_rotation/pallas_call | solution.py:354
  97.7 1.8 %copy.8 = bf16[96,2048]{1,0:T(8,128)(2,1)} copy(bf16[96,2048]{1,0:T(8,128)(2,1)} %filter_and_rotation.1) | data formatting | bytes 786432

commit v5 on v4

--- a/solution.py
+++ b/solution.py
@@ -9,6 +9,7 @@
 
 DEGREE = 3
 ROOT_ITERS = 4
+TILE = 256
 MESH = pl.DeviceIdType.MESH
 
 center = 7.0
@@ -43,14 +44,15 @@
 def kernel(
     n_dom, n_st, inner, with_tail,
     f_hbm, matrix_hbm, conn_hbm, surface_hbm, scale_ref, potential_hbm, out_ref,
-    matrix_ref, conn_ref, surface_ref, potential_ref, extended, history, totals, picks, surface_pick, pair, edge_out, edge_in, back_out, back_in,
+    matrix_ref, conn_ref, surface_ref, potential_ref, flat, extended, history, totals, picks, picks_down,
+    surface_pick, surface_down, masked, edge_out, edge_in, back_out, back_in,
     edge_send, edge_recv, back_send, back_recv, load_sems, *tail_refs,
 ):
     states, nodes = f_hbm.shape
     surf = surface_ref.shape[1]
     cells, node_cell = conn_ref.shape
     width = nodes + surf
-    tile = 256
+    tile = TILE
     me = lax.axis_index("dom")
     after, before = lax.rem(me + 1, n_dom), lax.rem(me + n_dom - 1, n_dom)
 
@@ -59,75 +61,90 @@
         pltpu.make_async_copy(src, dst, load_sems.at[index])
         for index, (src, dst) in enumerate([
             (conn_hbm, conn_ref), (surface_hbm, surface_ref),
-            (f_hbm, extended.at[:, pl.ds(0, nodes)]), (matrix_hbm, matrix_ref),
+            (f_hbm, flat), (matrix_hbm, matrix_ref),
             (potential_hbm, potential_ref),
         ])
     ]
     for load in loads:
         load.start()
 
-    def one_hot(ids, start):
-        columns = ids.shape[1]
-        node = lax.broadcasted_iota(jnp.int32, (tile, columns), 0).astype(jnp.bfloat16)
-        wanted = jnp.broadcast_to((ids - start).astype(jnp.bfloat16), (tile, columns))
-        one, zero = jnp.bfloat16(1), jnp.bfloat16(0)
-        return jnp.where(node == wanted, one, zero)
+    own_tiles, all_tiles = nodes // tile, width // tile
+    one, zero = jnp.bfloat16(1), jnp.bfloat16(0)
+
+    def places(ids):
+        return jnp.bitwise_and(ids, tile - 1)
+
+    def tiles_of(ids):
+        return jnp.right_shift(ids, 8)
+
+    def across(ids):
+        shape = (tile, ids.shape[1])
+        place = lax.broadcasted_iota(jnp.int32, shape, 0).astype(jnp.bfloat16)
+        wanted = jnp.broadcast_to(places(ids).astype(jnp.bfloat16), shape)
+        return jnp.where(place == wanted, one, zero)
+
+    def downwards(column):
+        shape = (column.shape[0], tile)
+        place = lax.broadcasted_iota(jnp.int32, shape, 1).astype(jnp.bfloat16)
+        wanted = jnp.broadcast_to(column, shape).astype(jnp.bfloat16)
+        return jnp.where(place == wanted, one, zero)
+
+    def gather(pick, ids, count):
+        found_all = jnp.dot(
+            extended[:count * states, :], pick, preferred_element_type=jnp.float32
+        )
+        place = jnp.broadcast_to(tiles_of(ids), (states, ids.shape[1]))
+        found = found_all[:states]
+        for t in range(1, count):
+            found = jnp.where(place == t, found_all[t * states:(t + 1) * states], found)
+        return found.astype(jnp.bfloat16)
+
+    def scatter(values, pick_down, ids, count, slot):
+        parts = halves(values)
+        lanes = pl.ds(slot * node_cell, ids.shape[1])
+        place = jnp.broadcast_to(tiles_of(ids).astype(jnp.bfloat16), parts.shape)
+        for t in range(count):
+            masked[pl.ds(t * 2 * states, 2 * states), lanes] = jnp.where(
+                place == jnp.bfloat16(t), parts, jnp.zeros_like(parts)
+            )
+        spread = jnp.dot(
+            masked[:count * 2 * states, lanes], pick_down, preferred_element_type=jnp.float32
+        )
+        for t in range(count):
+            low = t * 2 * states
+            totals[pl.ds(t * states, states), :] += (
+                spread[low:low + states] + spread[low + states:low + 2 * states]
+            )
 
     loads[0].wait()
-    ids_down = jnp.transpose(conn_ref[...].astype(jnp.float32))
+    places_down = jnp.transpose(places(conn_ref[...]).astype(jnp.float32))
     for cell in range(cells):
-        wanted = jnp.broadcast_to(ids_down[:, cell:cell + 1], (node_cell, tile))
-        lanes = lax.broadcasted_iota(jnp.int32, (node_cell, tile), 1).astype(jnp.bfloat16)
-        rows = pl.ds(cell * node_cell, node_cell)
-
-        def build_tile(index, carry):
-            start = index * tile
-            shifted = (wanted - start.astype(jnp.float32)).astype(jnp.bfloat16)
-            picks[rows, pl.ds(pl.multiple_of(start, tile), tile)] = jnp.where(
-                lanes == shifted, jnp.bfloat16(1), jnp.bfloat16(0)
-            )
-            return carry
-
-        lax.fori_loop(0, (nodes if cell < inner else width) // tile, build_tile, 0)
+        picks[cell] = across(conn_ref[pl.ds(cell, 1), :])
+        picks_down[cell] = downwards(places_down[:, cell:cell + 1])
     for load in loads[1:]:
         load.wait()
-    for start in range(0, nodes, tile):
-        surface_pick[pl.ds(start, tile), :] = one_hot(surface_ref[...], start)
-
-    def run_cells(first, last, extent):
-        count = last - first
-        gathered = []
-        for cell in range(first, last):
-            ids = conn_ref[pl.ds(cell, 1), :]
-            found = jnp.zeros((states, node_cell), jnp.float32)
-            for start in range(0, extent, tile):
-                found += jnp.dot(
-                    extended[:, start:start + tile], one_hot(ids, start),
-                    preferred_element_type=jnp.float32,
-                )
-            gathered.append(found.astype(jnp.bfloat16))
+    surface_ids = surface_ref[...]
+    surface_pick[...] = across(surface_ids)
+    surface_down[...] = jnp.transpose(surface_pick[...].astype(jnp.float32)).astype(jnp.bfloat16)
+    for t in range(own_tiles):
+        extended[pl.ds(t * states, states), :] = flat[:, t * tile:(t + 1) * tile]
+
+    def run_cells(first, last, count):
+        gathered = [
+            gather(picks[cell], conn_ref[pl.ds(cell, 1), :], count) for cell in range(first, last)
+        ]
         products = jnp.dot(
             jnp.concatenate(gathered, axis=0), matrix_ref[...], preferred_element_type=jnp.float32
         )
-        for index in range(count):
-            scaled = products[index * states:(index + 1) * states] * scale_ref[first + index]
-            pair[:, index * node_cell:(index + 1) * node_cell] = halves(scaled)
-        group = pl.ds(first * node_cell, count * node_cell)
-
-        for start in range(0, extent, tile):
-            columns = pl.ds(start, tile)
-            spread = jnp.dot(
-                pair[:, :count * node_cell], picks[group, columns],
-                preferred_element_type=jnp.float32,
-            )
-            totals[:, columns] += spread[:states] + spread[states:]
+        for index in range(last - first):
+            cell = first + index
+            scaled = products[index * states:(index + 1) * states] * scale_ref[cell]
+            scatter(scaled, picks_down[cell], conn_ref[pl.ds(cell, 1), :], count, index)
 
     pl.semaphore_wait(barrier, greetings)
 
     def one_step(step, carry):
-        edge_out[step] = jnp.dot(
-            extended[:, :nodes], surface_pick[...], preferred_element_type=jnp.float32
-        ).astype(jnp.bfloat16)
+        edge_out[step] = gather(surface_pick[...], surface_ids, own_tiles)
         edge = pltpu.make_async_remote_copy(
             src_ref=edge_out.at[step], dst_ref=edge_in.at[step],
             send_sem=edge_send.at[step], recv_sem=edge_recv.at[step],
@@ -135,46 +152,50 @@
         )
         edge.start()
         totals[...] = jnp.zeros_like(totals)
-        run_cells(0, inner // 2, nodes)
+        run_cells(0, inner // 2, own_tiles)
         edge.wait()
-        ghosts = edge_in[step]
-        extended[:, nodes:] = jnp.where(me == n_dom - 1, jnp.zeros_like(ghosts), ghosts)
-        run_cells(inner, cells, width)
-        back_out[step] = totals[:, nodes:]
+        for t in range(own_tiles, all_tiles):
+            ghosts = edge_in[step, :, (t - own_tiles) * tile:(t - own_tiles + 1) * tile]
+            extended[pl.ds(t * states, states), :] = jnp.where(
+                me == n_dom - 1, jnp.zeros_like(ghosts), ghosts
+            )
+        run_cells(inner, cells, all_tiles)
+        for t in range(own_tiles, all_tiles):
+            back_out[step, :, (t - own_tiles) * tile:(t - own_tiles + 1) * tile] = (
+                totals[pl.ds(t * states, states), :]
+            )
         back = pltpu.make_async_remote_copy(
             src_ref=back_out.at[step], dst_ref=back_in.at[step],
             send_sem=back_send.at[step], recv_sem=back_recv.at[step],
             device_id={"dom": after}, device_id_type=MESH,
         )
         back.start()
-        run_cells(inner // 2, inner, nodes)
+        run_cells(inner // 2, inner, own_tiles)
         back.wait()
         returned = back_in[step]
         returned = jnp.where(me == 0, jnp.zeros_like(returned), returned)
-        parts = halves(returned)
+        scatter(returned, surface_down[...], surface_ids, own_tiles, 0)
         first = step == 0
-        for start in range(0, nodes, tile):
-            columns = pl.ds(start, tile)
-            spread = lax.dot_general(
-                parts, surface_pick[columns, :], NT, preferred_element_type=jnp.float32
-            )
-            total = totals[:, columns] + (spread[:states] + spread[states:])
-            old = extended[:, columns]
+        for t in range(own_tiles):
+            rows = pl.ds(t * states, states)
+            old = extended[rows, :]
             newest = old.astype(jnp.float32)
-            image = total + potential_ref[:, columns] * newest
+            image = totals[rows, :] + potential_ref[:, t * tile:(t + 1) * tile] * newest
             shifted = (image - center * newest) / half_width
-            later = 2.0 * shifted - history[:, columns].astype(jnp.float32)
+            later = 2.0 * shifted - history[rows, :].astype(jnp.float32)
             fresh = jnp.where(first, shifted, later).astype(jnp.bfloat16)
-            history[:, columns] = old
-            extended[:, columns] = fresh
+            history[rows, :] = old
+            extended[rows, :] = fresh
         return carry
 
     history[...] = jnp.zeros_like(history)
     lax.fori_loop(0, DEGREE, one_step, 0)
+    for t in range(own_tiles):
+        flat[:, t * tile:(t + 1) * tile] = extended[pl.ds(t * states, states), :]
     if with_tail:
-        tail_part(n_dom, n_st, float(n_dom * nodes), states, nodes, extended, out_ref, *tail_refs)
+        tail_part(n_dom, n_st, float(n_dom * nodes), states, nodes, flat, out_ref, *tail_refs)
     else:
-        out_ref[...] = extended[:, :nodes]
+        out_ref[...] = flat[...]
 
 
 def product(left, right):
@@ -232,7 +253,7 @@
             for k in range(1, n_st)
         ]
 
-    full[band(q), :] = f_ref[:, :nodes]
+    full[band(q), :] = f_ref[...]
     for copy in slab:
         copy.wait()
 
@@ -361,12 +382,15 @@
             pltpu.VMEM((cells, node_cell), jnp.int32),
             pltpu.VMEM((1, surf), jnp.int32),
             pltpu.VMEM((1, nodes), f32),
-            pltpu.VMEM((states, nodes + surf), bf16),
             pltpu.VMEM((states, nodes), bf16),
-            pltpu.VMEM((states, nodes + surf), f32),
-            pltpu.VMEM((cells * node_cell, nodes + surf), bf16),
-            pltpu.VMEM((nodes, surf), bf16),
-            pltpu.VMEM((2 * states, cells * node_cell), bf16),
+            pltpu.VMEM(((nodes + surf) // TILE * states, TILE), bf16),
+            pltpu.VMEM((nodes // TILE * states, TILE), bf16),
+            pltpu.VMEM(((nodes + surf) // TILE * states, TILE), f32),
+            pltpu.VMEM((cells, TILE, node_cell), bf16),
+            pltpu.VMEM((cells, node_cell, TILE), bf16),
+            pltpu.VMEM((TILE, surf), bf16),
+            pltpu.VMEM((surf, TILE), bf16),
+            pltpu.VMEM(((nodes + surf) // TILE * 2 * states, cells * node_cell // 2), bf16),
             pltpu.VMEM((DEGREE, states, surf), bf16),
             pltpu.VMEM((DEGREE, states, surf), bf16),
             pltpu.VMEM((DEGREE, states, surf), f32),

time: 99.7 us -> 113 us (1.13)
  Pallas kernels: 97.7 us -> 111 us
    pallas_call x1, Pallas kernels: 97.7 us -> 111 us  [run_kernel(): pl.pallas_call(functools.partial(kernel, n_dom, n_st, cells - cells // 4,...]
where the time goes in v5:
time: 113 us
  Pallas kernels  111 us (98%)
  local copies, waits for them, and re-layouts  1.77 us (2%)
    pallas_call x1, Pallas kernels, run_kernel(): pl.pallas_call(functools.partial(kernel, n_dom, n_st, cells - cells // 4,...  111 us

profile of v5, /device:TPU:0, one launch (start us, length us, event | category | flops | bytes accessed | tf_op | source)
XLA Modules:
  0.0 112.6 jit_solution(4766013688898331661)
XLA Ops:
  0.0 110.8 %filter_and_rotation.1 = bf16[96,2048]{1,0:T(8,128)(2,1)} custom-call(bf16[96,2048]{1,0:T(8,128)(2,1)} %f_hbm.1, bf16[512,512]{1,0:T(8,128)(2,1)} %matrix_hbm.1, s32[16,512]{1,0:T(8,128)} %conn_hbm.1, s32[1,256]{1,0:T(1,128)} %surface_hbm.1, f32[16]{0:T(128)} %scale_ref.1, f32[1,2048]{1,0:T(1,128)} %bitcast.1), custom_call_target="tpu_custom_call" | custom-call | tf_op jit(solution)/shard_map/filter_and_rotation/pallas_call | solution.py:375
  110.8 1.8 %copy.8 = bf16[96,2048]{1,0:T(8,128)(2,1)} copy(bf16[96,2048]{1,0:T(8,128)(2,1)} %filter_and_rotation.1) | data formatting | bytes 786432

commit v6 on v5

--- a/solution.py
+++ b/solution.py
@@ -45,7 +45,7 @@
     n_dom, n_st, inner, with_tail,
     f_hbm, matrix_hbm, conn_hbm, surface_hbm, scale_ref, potential_hbm, out_ref,
     matrix_ref, conn_ref, surface_ref, potential_ref, flat, extended, history, totals, picks, picks_down,
-    surface_pick, surface_down, masked, edge_out, edge_in, back_out, back_in,
+    surface_pick, surface_down, pair, edge_out, edge_in, back_out, back_in,
     edge_send, edge_recv, back_send, back_recv, load_sems, *tail_refs,
 ):
     states, nodes = f_hbm.shape
@@ -83,11 +83,21 @@
         wanted = jnp.broadcast_to(places(ids).astype(jnp.bfloat16), shape)
         return jnp.where(place == wanted, one, zero)
 
-    def downwards(column):
+    def build_down(target, first, column, count):
         shape = (column.shape[0], tile)
         place = lax.broadcasted_iota(jnp.int32, shape, 1).astype(jnp.bfloat16)
-        wanted = jnp.broadcast_to(column, shape).astype(jnp.bfloat16)
-        return jnp.where(place == wanted, one, zero)
+        wanted = jnp.broadcast_to(column, shape)
+        rows = pl.ds(first, column.shape[0])
+
+        def build_tile(index, carry):
+            start = index * tile
+            shifted = (wanted - start.astype(jnp.float32)).astype(jnp.bfloat16)
+            target[rows, pl.ds(pl.multiple_of(start, tile), tile)] = jnp.where(
+                place == shifted, one, zero
+            )
+            return carry
+
+        lax.fori_loop(0, count, build_tile, 0)
 
     def gather(pick, ids, count):
         found_all = jnp.dot(
@@ -99,33 +109,22 @@
             found = jnp.where(place == t, found_all[t * states:(t + 1) * states], found)
         return found.astype(jnp.bfloat16)
 
-    def scatter(values, pick_down, ids, count, slot):
-        parts = halves(values)
-        lanes = pl.ds(slot * node_cell, ids.shape[1])
-        place = jnp.broadcast_to(tiles_of(ids).astype(jnp.bfloat16), parts.shape)
-        for t in range(count):
-            masked[pl.ds(t * 2 * states, 2 * states), lanes] = jnp.where(
-                place == jnp.bfloat16(t), parts, jnp.zeros_like(parts)
-            )
-        spread = jnp.dot(
-            masked[:count * 2 * states, lanes], pick_down, preferred_element_type=jnp.float32
-        )
-        for t in range(count):
-            low = t * 2 * states
-            totals[pl.ds(t * states, states), :] += (
-                spread[low:low + states] + spread[low + states:low + 2 * states]
-            )
-
     loads[0].wait()
-    places_down = jnp.transpose(places(conn_ref[...]).astype(jnp.float32))
+    ids_down = jnp.transpose(conn_ref[...].astype(jnp.float32))
     for cell in range(cells):
         picks[cell] = across(conn_ref[pl.ds(cell, 1), :])
-        picks_down[cell] = downwards(places_down[:, cell:cell + 1])
+        build_down(
+            picks_down, cell * node_cell, ids_down[:, cell:cell + 1],
+            own_tiles if cell < inner else all_tiles,
+        )
     for load in loads[1:]:
         load.wait()
     surface_ids = surface_ref[...]
     surface_pick[...] = across(surface_ids)
-    surface_down[...] = jnp.transpose(surface_pick[...].astype(jnp.float32)).astype(jnp.bfloat16)
+    surface_column = jnp.transpose(
+        jnp.broadcast_to(surface_ids.astype(jnp.float32), (8, surf))
+    )[:, :1]
+    build_down(surface_down, 0, surface_column, own_tiles)
     for t in range(own_tiles):
         extended[pl.ds(t * states, states), :] = flat[:, t * tile:(t + 1) * tile]
 
@@ -139,7 +138,15 @@
         for index in range(last - first):
             cell = first + index
             scaled = products[index * states:(index + 1) * states] * scale_ref[cell]
-            scatter(scaled, picks_down[cell], conn_ref[pl.ds(cell, 1), :], count, index)
+            pair[:, index * node_cell:(index + 1) * node_cell] = halves(scaled)
+        lanes = (last - first) * node_cell
+        group = pl.ds(first * node_cell, lanes)
+        for t in range(count):
+            columns = pl.ds(t * tile, tile)
+            spread = jnp.dot(
+                pair[:, :lanes], picks_down[group, columns], preferred_element_type=jnp.float32
+            )
+            totals[:, columns] += spread[:states] + spread[states:]
 
     pl.semaphore_wait(barrier, greetings)
 
@@ -160,10 +167,7 @@
                 me == n_dom - 1, jnp.zeros_like(ghosts), ghosts
             )
         run_cells(inner, cells, all_tiles)
-        for t in range(own_tiles, all_tiles):
-            back_out[step, :, (t - own_tiles) * tile:(t - own_tiles + 1) * tile] = (
-                totals[pl.ds(t * states, states), :]
-            )
+        back_out[step] = totals[:, nodes:]
         back = pltpu.make_async_remote_copy(
             src_ref=back_out.at[step], dst_ref=back_in.at[step],
             send_sem=back_send.at[step], recv_sem=back_recv.at[step],
@@ -174,13 +178,16 @@
         back.wait()
         returned = back_in[step]
         returned = jnp.where(me == 0, jnp.zeros_like(returned), returned)
-        scatter(returned, surface_down[...], surface_ids, own_tiles, 0)
+        parts = halves(returned)
         first = step == 0
         for t in range(own_tiles):
             rows = pl.ds(t * states, states)
             old = extended[rows, :]
             newest = old.astype(jnp.float32)
-            image = totals[rows, :] + potential_ref[:, t * tile:(t + 1) * tile] * newest
+            columns = pl.ds(t * tile, tile)
+            spread = jnp.dot(parts, surface_down[:, columns], preferred_element_type=jnp.float32)
+            total = totals[:, columns] + (spread[:states] + spread[states:])
+            image = total + potential_ref[:, columns] * newest
             shifted = (image - center * newest) / half_width
             later = 2.0 * shifted - history[rows, :].astype(jnp.float32)
             fresh = jnp.where(first, shifted, later).astype(jnp.bfloat16)
@@ -203,8 +210,11 @@
     left_low = (left - left_high.astype(jnp.float32)).astype(jnp.bfloat16)
     right_high = right.astype(jnp.bfloat16)
     right_low = (right - right_high.astype(jnp.float32)).astype(jnp.bfloat16)
-    dot = functools.partial(jnp.dot, preferred_element_type=jnp.float32)
-    return dot(left_high, right_high) + (dot(left_high, right_low) + dot(left_low, right_high))
+    return jnp.dot(
+        jnp.concatenate([left_high, left_high, left_low], axis=1),
+        jnp.concatenate([right_high, right_low, right_high], axis=0),
+        preferred_element_type=jnp.float32,
+    )
 
 
 def tail_part(
@@ -385,12 +395,12 @@
             pltpu.VMEM((states, nodes), bf16),
             pltpu.VMEM(((nodes + surf) // TILE * states, TILE), bf16),
             pltpu.VMEM((nodes // TILE * states, TILE), bf16),
-            pltpu.VMEM(((nodes + surf) // TILE * states, TILE), f32),
+            pltpu.VMEM((states, nodes + surf), f32),
             pltpu.VMEM((cells, TILE, node_cell), bf16),
-            pltpu.VMEM((cells, node_cell, TILE), bf16),
+            pltpu.VMEM((cells * node_cell, nodes + surf), bf16),
             pltpu.VMEM((TILE, surf), bf16),
-            pltpu.VMEM((surf, TILE), bf16),
-            pltpu.VMEM(((nodes + surf) // TILE * 2 * states, cells * node_cell // 2), bf16),
+            pltpu.VMEM((surf, nodes), bf16),
+            pltpu.VMEM((2 * states, cells * node_cell // 2), bf16),
             pltpu.VMEM((DEGREE, states, surf), bf16),
             pltpu.VMEM((DEGREE, states, surf), bf16),
             pltpu.VMEM((DEGREE, states, surf), f32),

time: 113 us -> 92.6 us (0.82)
  Pallas kernels: 111 us -> 90.7 us
    pallas_call x1, Pallas kernels: 111 us -> 90.7 us  [run_kernel(): pl.pallas_call(functools.partial(kernel, n_dom, n_st, cells - cells // 4,...]
where the time goes in v6:
time: 92.6 us; the launch traced here: 92.4 us
  Pallas kernels  90.7 us (98%)
  local copies, waits for them, and re-layouts  1.77 us (2%)
    pallas_call x1, Pallas kernels, run_kernel(): pl.pallas_call(functools.partial(kernel, n_dom, n_st, cells - cells // 4,...  90.7 us

profile of v6, /device:TPU:0, one launch (start us, length us, event | category | flops | bytes accessed | tf_op | source)
XLA Modules:
  0.0 92.4 jit_solution(15057253712454522000)
XLA Ops:
  0.0 90.7 %filter_and_rotation.1 = bf16[96,2048]{1,0:T(8,128)(2,1)} custom-call(bf16[96,2048]{1,0:T(8,128)(2,1)} %f_hbm.1, bf16[512,512]{1,0:T(8,128)(2,1)} %matrix_hbm.1, s32[16,512]{1,0:T(8,128)} %conn_hbm.1, s32[1,256]{1,0:T(1,128)} %surface_hbm.1, f32[16]{0:T(128)} %scale_ref.1, f32[1,2048]{1,0:T(1,128)} %bitcast.1), custom_call_target="tpu_custom_call" | custom-call | tf_op jit(solution)/shard_map/filter_and_rotation/pallas_call | solution.py:385
  90.7 1.8 %copy.8 = bf16[96,2048]{1,0:T(8,128)(2,1)} copy(bf16[96,2048]{1,0:T(8,128)(2,1)} %filter_and_rotation.1) | data formatting | bytes 786432
